TPU v7x, 128 devices: a whole 4x4x4 slice. The times are simulated.
128 devices in a mesh: section: 2 (over y_lo), dp: 16 (over x, z), tensor: 4 (over y_hi, core).
Axes of the slice: x: 4, y: 4 (y_hi: 2, y_lo: 2; y = y_hi * 2 + y_lo), z: 4, core: 2. Of those that a mesh axis runs over, the one named last changes fastest.
Arguments:
- embedded: bfloat16 [2, 2, 4096, 1024], P('section', None, ('dp', 'tensor')), may hold values from -6 to 6
- cotangent: bfloat16 [2, 2, 4096, 1024], P('section', None, ('dp', 'tensor')), may hold values from -6 to 6
- lengths: int32 [2, 2, 16, 8], P(None, None, 'dp'), may hold values from 1 to 194, 256 in all within a row
- attn_qkv: bfloat16 [2, 1024, 3072], P('section', 'dp', 'tensor'), may hold values from -0.1875 to 0.1875
- attn_out: bfloat16 [2, 1024, 1024], P('section', 'tensor', 'dp'), may hold values from -0.75 to 0.75
- ffn_up: bfloat16 [2, 1024, 4096], P('section', 'dp', 'tensor'), may hold values from -0.1875 to 0.1875
- ffn_down: bfloat16 [2, 4096, 1024], P('section', 'tensor', 'dp'), may hold values from -0.1875 to 0.1875
- norm_gain: bfloat16 [2, 3, 1024], P('section', None, 'dp'), may hold values from 0.5 to 1.5
- norm_bias: bfloat16 [2, 3, 1024], P('section', None, 'dp'), may hold values from -0.5 to 0.5
- cross_query: bfloat16 [1024, 1024], P(('section', 'dp'), 'tensor'), may hold values from -0.1875 to 0.1875
- cross_kv: bfloat16 [1024, 2048], P(('section', 'dp'), 'tensor'), may hold values from -0.1875 to 0.1875
- cross_out: bfloat16 [1024, 1024], P('tensor', ('section', 'dp')), may hold values from -0.75 to 0.75
Outputs:
- outputs: bfloat16 [2, 2, 4096, 1024], P('section', None, ('dp', 'tensor'))
- g_embedded: float32 [2, 2, 4096, 1024], P('section', None, ('dp', 'tensor'))
- g_attn_qkv: float32 [2, 1024, 3072], P('section', 'dp', 'tensor')
- g_attn_out: float32 [2, 1024, 1024], P('section', 'tensor', 'dp')
- g_ffn_up: float32 [2, 1024, 4096], P('section', 'dp', 'tensor')
- g_ffn_down: float32 [2, 4096, 1024], P('section', 'tensor', 'dp')
- g_norm_gain: float32 [2, 3, 1024], P('section', None, 'dp')
- g_norm_bias: float32 [2, 3, 1024], P('section', None, 'dp')
- g_cross_query: float32 [1024, 1024], P(('section', 'dp'), 'tensor')
- g_cross_kv: float32 [1024, 2048], P(('section', 'dp'), 'tensor')
- g_cross_out: float32 [1024, 1024], P('tensor', ('section', 'dp'))
Inputs may be any that keep to these rules, and one draw needn't show every extreme that they name: The 8 pair lengths of each row sum to 256, and every row has one pair of exactly 194 tokens.
All inputs are finite; a program needn't handle non-finite values.
Results may differ from a plain program's by a relative error of at most 0.02.
Values may be sent and summed in bfloat16 or wider, within the bound.
No kernel may reach another device: no remote copies, remote signals or barrier semaphores. Data moves between devices by JAX's collectives and lax.ppermute only.
A program may use at most 128 MiB of HBM per device.

v0:
```python
import jax
import jax.numpy as jnp
from jax import lax
from jax.sharding import PartitionSpec as P

HEAD_DIM = 64
ROW_LEN = 256


EPSILON = 1e-05
NEGATIVE = -1000000000.0
SCALING = 0.125
GELU_COEF = 0.7978845608028654
BFLOAT = jnp.bfloat16
FLOAT = jnp.float32


def from_behind(block, axis, distance):
    devices = range(lax.axis_size(axis))
    route = [(i - distance, i) for i in devices if i - distance in devices]
    return lax.ppermute(block, axis, route)


def gelu_tanh(values):
    return (
        0.5 * values * (1.0 + jnp.tanh(GELU_COEF * (values + 0.044715 * values * values * values)))
    )


def layer_norm(values, gain, offset):
    centred = values - jnp.mean(values, axis=-1, keepdims=True)
    inverse = lax.rsqrt(jnp.mean(centred * centred, axis=-1, keepdims=True) + EPSILON)
    normed = centred * inverse
    return (normed * gain + offset, normed, inverse)


def norm_backward(grad_out, normed, inverse, gain):
    scaled = grad_out * gain
    inner = (
        scaled
        - jnp.mean(scaled, axis=-1, keepdims=True)
        - normed * jnp.mean(scaled * normed, axis=-1, keepdims=True)
    )
    return (inverse * inner, jnp.sum(grad_out * normed, axis=0), jnp.sum(grad_out, axis=0))


def segment_ids(lengths_row):
    ends = jnp.cumsum(lengths_row)
    positions = jnp.arange(ROW_LEN, dtype=jnp.int32)
    return jnp.sum((positions[:, None] >= ends[None, :]).astype(jnp.int32), axis=1)


def apply_projection(left, right):
    return jnp.dot(left, right, preferred_element_type=FLOAT)


def project_left(left, right):
    return lax.dot_general(left, right, (((0,), (0,)), ((), ())), preferred_element_type=FLOAT)


def project_right(left, right):
    return lax.dot_general(left, right, (((1,), (1,)), ((), ())), preferred_element_type=FLOAT)


def run_if(flag, function, *operands):
    results = function(*operands)
    return jax.tree.map(lambda leaf: jnp.where(flag, leaf, jnp.zeros_like(leaf)), results)


def gather_rows(values):
    return lax.all_gather(values, "tensor", axis=0, tiled=True)


def sum_rows(values):
    return lax.psum_scatter(values, "tensor", scatter_dimension=0, tiled=True)


def attend_forward(query_heads, key_heads, value_heads, allowed):
    scores = (
        jnp.einsum("qhd,khd->hqk", query_heads, key_heads, preferred_element_type=FLOAT) * SCALING
    )
    scores = jnp.where(allowed[None], scores, NEGATIVE)
    highest = jnp.max(scores, axis=-1, keepdims=True)
    expo_scores = jnp.exp(scores - highest)
    totals = jnp.sum(expo_scores, axis=-1, keepdims=True)
    weights_low = (expo_scores / totals).astype(BFLOAT)
    mixed = jnp.einsum("hqk,khd->qhd", weights_low, value_heads, preferred_element_type=FLOAT)
    return (mixed.reshape(mixed.shape[0], -1).astype(BFLOAT), highest + jnp.log(totals))


def attend_backward(query_heads, key_heads, value_heads, allowed, log_total, grad_mixed):
    scores = (
        jnp.einsum("qhd,khd->hqk", query_heads, key_heads, preferred_element_type=FLOAT) * SCALING
    )
    scores = jnp.where(allowed[None], scores, NEGATIVE)
    weights_full = jnp.exp(scores - log_total)
    grad_values = jnp.einsum(
        "hqk,qhd->khd", weights_full.astype(BFLOAT), grad_mixed, preferred_element_type=FLOAT
    )
    grad_weights = jnp.einsum("qhd,khd->hqk", grad_mixed, value_heads, preferred_element_type=FLOAT)
    grad_scores = weights_full * (
        grad_weights - jnp.sum(weights_full * grad_weights, axis=-1, keepdims=True)
    )
    grad_scores = grad_scores.astype(BFLOAT)
    grad_queries = (
        jnp.einsum("hqk,khd->qhd", grad_scores, key_heads, preferred_element_type=FLOAT) * SCALING
    )
    grad_keys = (
        jnp.einsum("hqk,qhd->khd", grad_scores, query_heads, preferred_element_type=FLOAT) * SCALING
    )
    return (grad_queries, grad_keys, grad_values)


def self_forward(rows, weight_qkv, weight_out, allowed):
    length = rows.shape[0]
    projected = apply_projection(rows, weight_qkv).astype(BFLOAT)
    heads = projected.reshape(length, -1, 3, HEAD_DIM)
    mixed, log_total = attend_forward(heads[:, :, 0], heads[:, :, 1], heads[:, :, 2], allowed)
    return (apply_projection(mixed, weight_out), projected, mixed, log_total)


def self_attention_backward(
    rows, projected, mixed, log_total, weight_qkv, weight_out, allowed, grad_rows
):
    length = rows.shape[0]
    grad_weight_out = project_left(mixed, grad_rows)
    grad_mixed = project_right(grad_rows, weight_out).astype(BFLOAT)
    heads = projected.reshape(length, -1, 3, HEAD_DIM)
    grad_q, grad_k, grad_v = attend_backward(
        heads[:, :, 0],
        heads[:, :, 1],
        heads[:, :, 2],
        allowed,
        log_total,
        grad_mixed.reshape(length, -1, HEAD_DIM),
    )
    grad_projected = jnp.stack([grad_q, grad_k, grad_v], axis=2).reshape(length, -1).astype(BFLOAT)
    return (
        project_right(grad_projected, weight_qkv),
        project_left(rows, grad_projected),
        grad_weight_out,
    )


def cross_forward(rows, memory_rows, weight_query, weight_keyval, weight_cross, allowed):
    length = rows.shape[0]
    queries = apply_projection(rows, weight_query).astype(BFLOAT)
    keyvals = apply_projection(memory_rows, weight_keyval).astype(BFLOAT)
    pair_heads = keyvals.reshape(length, -1, 2, HEAD_DIM)
    mixed, log_total = attend_forward(
        queries.reshape(length, -1, HEAD_DIM), pair_heads[:, :, 0], pair_heads[:, :, 1], allowed
    )
    return (apply_projection(mixed, weight_cross), queries, keyvals, mixed, log_total)


def cross_backward(
    rows,
    memory_rows,
    queries,
    keyvals,
    mixed,
    log_total,
    weight_query,
    weight_keyval,
    weight_cross,
    allowed,
    grad_rows,
):
    length = rows.shape[0]
    grad_weight_cross = project_left(mixed, grad_rows)
    grad_mixed = project_right(grad_rows, weight_cross).astype(BFLOAT)
    pair_heads = keyvals.reshape(length, -1, 2, HEAD_DIM)
    grad_q, grad_k, grad_v = attend_backward(
        queries.reshape(length, -1, HEAD_DIM),
        pair_heads[:, :, 0],
        pair_heads[:, :, 1],
        allowed,
        log_total,
        grad_mixed.reshape(length, -1, HEAD_DIM),
    )
    grad_queries = grad_q.reshape(length, -1).astype(BFLOAT)
    grad_keyvals = jnp.stack([grad_k, grad_v], axis=2).reshape(length, -1).astype(BFLOAT)
    return (
        project_right(grad_queries, weight_query),
        project_right(grad_keyvals, weight_keyval),
        project_left(rows, grad_queries),
        project_left(memory_rows, grad_keyvals),
        grad_weight_cross,
    )


def ffn_forward(rows, weight_up, weight_down):
    hidden = apply_projection(rows, weight_up)
    activated = gelu_tanh(hidden).astype(BFLOAT)
    return (apply_projection(activated, weight_down), hidden, activated)


def ffn_backward(rows, hidden, activated, weight_up, weight_down, grad_rows):
    grad_weight_down = project_left(activated, grad_rows)
    grad_activated = project_right(grad_rows, weight_down)
    slope = jax.vjp(gelu_tanh, hidden)[1]
    grad_hidden = slope(grad_activated)[0].astype(BFLOAT)
    return (
        project_right(grad_hidden, weight_up),
        project_left(rows, grad_hidden),
        grad_weight_down,
    )


def shards(
    embedded,
    cotangent,
    lengths,
    attn_qkv,
    attn_out,
    ffn_up,
    ffn_down,
    norm_gain,
    norm_bias,
    cross_query,
    cross_kv,
    cross_out,
):
    section_index = lax.axis_index("section")
    is_decoder = section_index == 1
    encoder_weight = (1 - section_index).astype(FLOAT)
    microbatch_count = embedded.shape[1]

    def fetch():
        whole_section = (
            lax.all_gather(attn_qkv, "dp", axis=1, tiled=True),
            lax.all_gather(attn_out, "dp", axis=2, tiled=True),
            lax.all_gather(ffn_up, "dp", axis=1, tiled=True),
            lax.all_gather(ffn_down, "dp", axis=2, tiled=True),
            lax.all_gather(norm_gain, "dp", axis=2, tiled=True),
            lax.all_gather(norm_bias, "dp", axis=2, tiled=True),
        )
        whole_cross = (
            lax.all_gather(cross_query, ("section", "dp"), axis=0, tiled=True),
            lax.all_gather(cross_kv, ("section", "dp"), axis=0, tiled=True),
            lax.all_gather(cross_out, ("section", "dp"), axis=1, tiled=True),
        )
        members = tuple((member[0] for member in whole_section))
        return (members, whole_cross)

    def masks_for(clipped):
        source_lengths = lax.dynamic_index_in_dim(lengths[0], clipped, 0, keepdims=False)[0]
        target_lengths = lax.dynamic_index_in_dim(lengths[1], clipped, 0, keepdims=False)[0]
        source_pair = segment_ids(source_lengths)
        target_pair = segment_ids(target_lengths)
        own_pair = jnp.where(is_decoder, target_pair, source_pair)
        positions = jnp.arange(ROW_LEN, dtype=jnp.int32)
        ordered = (positions[None, :] <= positions[:, None]) | jnp.logical_not(is_decoder)
        allowed_self = (own_pair[:, None] == own_pair[None, :]) & ordered
        allowed_cross = target_pair[:, None] == source_pair[None, :]
        return (allowed_self, allowed_cross)

    memory_in = jnp.zeros(embedded.shape[2:], BFLOAT)
    outputs = jnp.zeros(embedded.shape[1:], BFLOAT)
    saved_activations = []
    for iteration_index in range(microbatch_count + 1):
        micro_index = iteration_index - section_index
        is_valid = (micro_index >= 0) & (micro_index < microbatch_count)
        clipped = jnp.clip(micro_index, 0, microbatch_count - 1)
        allowed_self, allowed_cross = masks_for(clipped)
        values = lax.dynamic_index_in_dim(embedded[0], clipped, 0, keepdims=False).astype(FLOAT)
        forward_members, forward_whole_cross = fetch()
        (
            forward_weight_qkv,
            forward_weight_out,
            forward_weight_up,
            forward_weight_down,
            forward_norm_gains,
            forward_norm_offsets,
        ) = forward_members
        forward_norm_gains = forward_norm_gains.astype(FLOAT)
        forward_norm_offsets = forward_norm_offsets.astype(FLOAT)
        forward_weight_query, forward_weight_keyval, forward_weight_cross = forward_whole_cross
        normed_one, forward_unit_one, forward_inverse_one = layer_norm(
            values, forward_norm_gains[0], forward_norm_offsets[0]
        )
        forward_rows_one = gather_rows(normed_one.astype(BFLOAT))
        part_one, forward_projected, forward_mixed_one, forward_total_one = run_if(
            is_valid,
            self_forward,
            forward_rows_one,
            forward_weight_qkv,
            forward_weight_out,
            allowed_self,
        )
        after_self = values + sum_rows(part_one)
        forward_memory_rows = gather_rows(memory_in)
        normed_two, forward_unit_two, forward_inverse_two = layer_norm(
            after_self, forward_norm_gains[1], forward_norm_offsets[1]
        )
        forward_rows_two = gather_rows(normed_two.astype(BFLOAT))
        part_two, forward_queries, forward_keyvals, forward_mixed_two, forward_total_two = run_if(
            is_valid & is_decoder,
            cross_forward,
            forward_rows_two,
            forward_memory_rows,
            forward_weight_query,
            forward_weight_keyval,
            forward_weight_cross,
            allowed_cross,
        )
        after_cross = after_self + sum_rows(part_two)
        normed_three, forward_unit_three, forward_inverse_three = layer_norm(
            after_cross, forward_norm_gains[2], forward_norm_offsets[2]
        )
        forward_rows_three = gather_rows(normed_three.astype(BFLOAT))
        part_three, forward_hidden, forward_activated = run_if(
            is_valid, ffn_forward, forward_rows_three, forward_weight_up, forward_weight_down
        )
        after_ffn = after_cross + sum_rows(part_three)
        normed_memory, forward_unit_memory, forward_inverse_memory = layer_norm(
            after_ffn, forward_norm_gains[1], forward_norm_offsets[1]
        )
        memory_out = normed_memory.astype(BFLOAT)
        result = jnp.where(is_decoder, after_ffn.astype(BFLOAT), memory_out)
        forward_saved_activation = (
            forward_unit_one,
            forward_inverse_one,
            forward_rows_one,
            forward_projected,
            forward_mixed_one,
            forward_total_one,
            forward_unit_two,
            forward_inverse_two,
            forward_rows_two,
            forward_memory_rows,
            forward_queries,
            forward_keyvals,
            forward_mixed_two,
            forward_total_two,
            forward_unit_three,
            forward_inverse_three,
            forward_rows_three,
            forward_hidden,
            forward_activated,
            forward_unit_memory,
            forward_inverse_memory,
        )
        result, memory_out, saved_activation = (result, memory_out, forward_saved_activation)
        previous = lax.dynamic_index_in_dim(outputs, clipped, 0, keepdims=False)
        outputs = lax.dynamic_update_index_in_dim(
            outputs, jnp.where(is_valid, result, previous), clipped, 0
        )
        saved_activations.append(saved_activation)
        if iteration_index < microbatch_count:
            memory_in = from_behind(memory_out, "section", 1)
    memory_grad_in = jnp.zeros(embedded.shape[2:], FLOAT)
    grad_embedded = jnp.zeros(embedded.shape[1:], FLOAT)
    section_total = None
    cross_total = None
    for iteration_index in range(microbatch_count + 1):
        micro_index = iteration_index - 1 + section_index
        is_valid = (micro_index >= 0) & (micro_index < microbatch_count)
        clipped = jnp.clip(micro_index, 0, microbatch_count - 1)
        allowed_self, allowed_cross = masks_for(clipped)
        following_value = saved_activations[min(iteration_index + 1, microbatch_count)]
        preceding_value = saved_activations[max(iteration_index - 1, 0)]
        saved_activation = jax.tree.map(
            lambda later_leaf, earlier_leaf: jnp.where(is_decoder, later_leaf, earlier_leaf),
            following_value,
            preceding_value,
        )
        grad_out = lax.dynamic_index_in_dim(cotangent[0], clipped, 0, keepdims=False).astype(FLOAT)
        backward_grad_out = grad_out
        backward_memory_grad_in = memory_grad_in
        (
            unit_one,
            inverse_one,
            rows_one,
            projected,
            mixed_one,
            total_one,
            unit_two,
            inverse_two,
            rows_two,
            memory_rows,
            queries,
            keyvals,
            mixed_two,
            total_two,
            unit_three,
            inverse_three,
            rows_three,
            hidden,
            activated,
            unit_memory,
            inverse_memory,
        ) = saved_activation
        backward_members, backward_whole_cross = fetch()
        weight_qkv, weight_out, weight_up, weight_down, norm_gains, norm_offsets = backward_members
        norm_gains = norm_gains.astype(FLOAT)
        weight_query, weight_keyval, weight_cross = backward_whole_cross
        valid_scale = is_valid.astype(FLOAT)
        backward_grad_out = backward_grad_out * valid_scale
        backward_memory_grad_in = backward_memory_grad_in * valid_scale
        grad_memory_norm, gain_memory, offset_memory = norm_backward(
            backward_grad_out + backward_memory_grad_in, unit_memory, inverse_memory, norm_gains[1]
        )
        grad_ffn = jnp.where(is_decoder, backward_grad_out, grad_memory_norm)
        rows_grad_three = gather_rows(grad_ffn.astype(BFLOAT))
        input_three, grad_up, grad_down = run_if(
            is_valid,
            ffn_backward,
            rows_three,
            hidden,
            activated,
            weight_up,
            weight_down,
            rows_grad_three,
        )
        norm_three, gain_three, offset_three = norm_backward(
            sum_rows(input_three), unit_three, inverse_three, norm_gains[2]
        )
        grad_cross_path = grad_ffn + norm_three
        rows_grad_two = gather_rows(grad_cross_path.astype(BFLOAT))
        input_two, memory_part, grad_query, grad_keyval, grad_cross = run_if(
            is_valid & is_decoder,
            cross_backward,
            rows_two,
            memory_rows,
            queries,
            keyvals,
            mixed_two,
            total_two,
            weight_query,
            weight_keyval,
            weight_cross,
            allowed_cross,
            rows_grad_two,
        )
        summed_two = lax.psum_scatter(input_two, "tensor", scatter_dimension=0, tiled=True)
        memory_grad_out = lax.psum_scatter(memory_part, "tensor", scatter_dimension=0, tiled=True)
        norm_two, gain_two, offset_two = norm_backward(
            summed_two, unit_two, inverse_two, norm_gains[1]
        )
        grad_self_path = grad_cross_path + norm_two
        rows_grad_one = gather_rows(grad_self_path.astype(BFLOAT))
        input_one, grad_qkv, grad_attn_out = run_if(
            is_valid,
            self_attention_backward,
            rows_one,
            projected,
            mixed_one,
            total_one,
            weight_qkv,
            weight_out,
            allowed_self,
            rows_grad_one,
        )
        norm_one, gain_one, offset_one = norm_backward(
            sum_rows(input_one), unit_one, inverse_one, norm_gains[0]
        )
        grad_input = grad_self_path + norm_one
        gain_grads = jnp.stack([gain_one, gain_two + encoder_weight * gain_memory, gain_three])
        offset_grads = jnp.stack(
            [offset_one, offset_two + encoder_weight * offset_memory, offset_three]
        )
        section_grads = (grad_qkv, grad_attn_out, grad_up, grad_down, gain_grads, offset_grads)
        cross_grads = (grad_query, grad_keyval, grad_cross)
        grad_input, memory_grad_out, section_grads, cross_grads = (
            grad_input,
            memory_grad_out,
            section_grads,
            cross_grads,
        )
        previous = lax.dynamic_index_in_dim(grad_embedded, clipped, 0, keepdims=False)
        grad_embedded = lax.dynamic_update_index_in_dim(
            grad_embedded, jnp.where(is_valid, grad_input, previous), clipped, 0
        )
        grad_qkv, grad_attn_out, grad_up, grad_down, gain_grads, offset_grads = section_grads
        grad_query, grad_keyval, grad_cross = cross_grads
        section_part = (
            lax.psum_scatter(grad_qkv, "dp", scatter_dimension=0, tiled=True),
            lax.psum_scatter(grad_attn_out, "dp", scatter_dimension=1, tiled=True),
            lax.psum_scatter(grad_up, "dp", scatter_dimension=0, tiled=True),
            lax.psum_scatter(grad_down, "dp", scatter_dimension=1, tiled=True),
            lax.psum_scatter(gain_grads, "dp", scatter_dimension=1, tiled=True),
            lax.psum_scatter(offset_grads, "dp", scatter_dimension=1, tiled=True),
        )
        cross_part = (
            lax.psum_scatter(grad_query, ("section", "dp"), scatter_dimension=0, tiled=True),
            lax.psum_scatter(grad_keyval, ("section", "dp"), scatter_dimension=0, tiled=True),
            lax.psum_scatter(grad_cross, ("section", "dp"), scatter_dimension=1, tiled=True),
        )
        section_total = (
            section_part
            if section_total is None
            else jax.tree.map(jnp.add, section_total, section_part)
        )
        cross_total = (
            cross_part if cross_total is None else jax.tree.map(jnp.add, cross_total, cross_part)
        )
        if iteration_index < microbatch_count:
            memory_grad_in = from_behind(memory_grad_out, "section", -1)
    gain_shard, offset_shard = lax.psum((section_total[4], section_total[5]), "tensor")
    return (
        outputs[None],
        grad_embedded[None],
        section_total[0][None],
        section_total[1][None],
        section_total[2][None],
        section_total[3][None],
        gain_shard[None],
        offset_shard[None],
        cross_total[0],
        cross_total[1],
        cross_total[2],
    )


def solution(mesh):
    return jax.shard_map(
        shards,
        mesh=mesh,
        in_specs=(
            P("section", None, ("dp", "tensor"), None),
            P("section", None, ("dp", "tensor"), None),
            P(None, None, "dp", None),
            P("section", "dp", "tensor"),
            P("section", "tensor", "dp"),
            P("section", "dp", "tensor"),
            P("section", "tensor", "dp"),
            P("section", None, "dp"),
            P("section", None, "dp"),
            P(("section", "dp"), "tensor"),
            P(("section", "dp"), "tensor"),
            P("tensor", ("section", "dp")),
        ),
        out_specs=(
            P("section", None, ("dp", "tensor"), None),
            P("section", None, ("dp", "tensor"), None),
            P("section", "dp", "tensor"),
            P("section", "tensor", "dp"),
            P("section", "dp", "tensor"),
            P("section", "tensor", "dp"),
            P("section", None, "dp"),
            P("section", None, "dp"),
            P(("section", "dp"), "tensor"),
            P(("section", "dp"), "tensor"),
            P("tensor", ("section", "dp")),
        ),
        check_vma=False,
    )
```

profile of v0, /device:TPU:0, one launch (start us, length us, event | category | flops | bytes accessed | tf_op | source)
XLA Modules:
  0.0 2113.4 jit_solution(5953270964089179096)
XLA Ops:
  10.8 25.7 %all_gather.58 = bf16[1,3,1024]{1,0,2:T(2,128)(2,1)S(1)} all-gather(bf16[1,3,64]{1,0,2:T(2,128)(2,1)S(1)} %copy.349), channel_id=1, replica_groups=mesh['section'=2,'dp'=16,'tensor'=4] {'dp'}, dimensions={2}, use_global_device_ids=true | all-gather | bytes 6528 | tf_op jit(solution)/shard_map/all_gather | solution.py:235
  37.1 10.4 slice_reduce_fusion.1
  47.6 23.7 %all_gather.59 = bf16[1,3,1024]{1,0,2:T(2,128)(2,1)S(1)} all-gather(bf16[1,3,64]{1,0,2:T(2,128)(2,1)S(1)} %copy.350), channel_id=1, replica_groups=mesh['section'=2,'dp'=16,'tensor'=4] {'dp'}, dimensions={2}, use_global_device_ids=true | all-gather | bytes 6528 | tf_op jit(solution)/shard_map/all_gather | solution.py:236
  71.8 10.4 slice_reduce_fusion
  83.5 8.7 all_gather.70
  92.2 8.8 all_gather.145
  101.0 9.2 all_gather.60
  114.5 24.2 %all_gather.62 = bf16[1,256,1024]{1,2,0:T(8,128)(2,1)S(1)} all-gather(bf16[1,256,64]{1,2,0:T(8,128)(2,1)S(1)} %copy-done.159), channel_id=1, replica_groups=mesh['section'=2,'dp'=16,'tensor'=4] {'dp'}, dimensions={2}, use_global_device_ids=true | all-gather | bytes 557056 | tf_op jit(solution)/shard_map/all_gather | solution.py:232
  158.7 81.1 %all_gather.65 = bf16[1024,256]{1,0:T(8,128)(2,1)S(1)} all-gather(bf16[32,256]{1,0:T(8,128)(2,1)S(1)} %copy-done.192), channel_id=1, replica_groups=mesh['section'=2,'dp'=16,'tensor'=4] {'section','dp'}, dimensions={0}, use_global_device_ids=true | all-gather | bytes 540672 | tf_op jit(solution)/shard_map/all_gather | solution.py:239
  239.8 78.4 %all_gather.66 = bf16[256,1024]{0,1:T(8,128)(2,1)S(1)} all-gather(bf16[256,32]{0,1:T(8,128)(2,1)S(1)} %copy-done.193), channel_id=1, replica_groups=mesh['section'=2,'dp'=16,'tensor'=4] {'section','dp'}, dimensions={1}, use_global_device_ids=true | all-gather | bytes 540672 | tf_op jit(solution)/shard_map/all_gather | solution.py:241
  323.5 8.3 all_gather.64
  337.2 27.6 %reduce-scatter.42.cloned.1.call-done = f32[64,1024]{1,0:T(8,128)} async-done(((f32[256,1024]{1,0:T(8,128)}), f32[64,1024]{1,0:T(8,128)}) %reduce-scatter.42.cloned.1.call-update) | async-done | bytes 262160 | tf_op jit(solution)/shard_map/reduce_scatter | solution.py:75
  375.0 36.6 %all-gather.9.cloned.1.call-done = bf16[1,1024,1024]{2,1,0:T(8,128)(2,1)} async-done(((bf16[1,64,1024]{2,1,0:T(8,128)(2,1)}), bf16[1,1024,1024]{2,1,0:T(8,128)(2,1)}) %all-gather.9.cloned.1.call-update) | async-done | bytes 2097168 | tf_op jit(solution)/shard_map/all_gather | solution.py:233
  414.9 43.4 %all-gather.11.cloned.1.call-done = bf16[1,1024,1024]{1,2,0:T(8,128)(2,1)} async-done(((bf16[1,1024,64]{1,2,0:T(8,128)(2,1)}), bf16[1,1024,1024]{1,2,0:T(8,128)(2,1)}) %all-gather.11.cloned.1.call-update) | async-done | bytes 2097168 | tf_op jit(solution)/shard_map/all_gather | solution.py:234
  463.0 30.4 %reduce-scatter.44.cloned.1.call-done = f32[64,1024]{1,0:T(8,128)} async-done(((f32[256,1024]{1,0:T(8,128)}), f32[64,1024]{1,0:T(8,128)}) %reduce-scatter.44.cloned.1.call-update) | async-done | bytes 262160 | tf_op jit(solution)/shard_map/reduce_scatter | solution.py:75
  498.6 8.9 all_gather.143
  508.5 9.0 all_gather.142
  522.3 31.7 %reduce-scatter.48.cloned.1.call-done = f32[64,1024]{1,0:T(8,128)} async-done(((f32[256,1024]{1,0:T(8,128)}), f32[64,1024]{1,0:T(8,128)}) %reduce-scatter.48.cloned.1.call-update) | async-done | bytes 262160 | tf_op jit(solution)/shard_map/reduce_scatter | solution.py:75
  556.7 8.4 all_gather.144
  569.6 31.3 %reduce-scatter.50.cloned.1.call-done = f32[64,1024]{1,0:T(8,128)} async-done(((f32[256,1024]{1,0:T(8,128)}), f32[64,1024]{1,0:T(8,128)}) %reduce-scatter.50.cloned.1.call-update) | async-done | bytes 262160 | tf_op jit(solution)/shard_map/reduce_scatter | solution.py:75
  625.3 9.6 all_gather.147
  637.3 8.8 all_gather.146
  662.5 24.0 %reduce-scatter.54.cloned.1.call-done = f32[64,1024]{1,0:T(8,128)} async-done(((f32[256,1024]{1,0:T(8,128)}), f32[64,1024]{1,0:T(8,128)}) %reduce-scatter.54.cloned.1.call-update) | async-done | bytes 262160 | tf_op jit(solution)/shard_map/reduce_scatter | solution.py:75
  691.3 8.4 all_gather.148
  707.3 9.5 all_gather.150
  722.3 13.2 reduce-scatter.56.cloned.1.call-done
  737.9 31.4 %reduce-scatter.64.cloned.1.call-done = f32[64,1024]{1,0:T(8,128)} async-done(((f32[256,1024]{1,0:T(8,128)}), f32[64,1024]{1,0:T(8,128)}) %reduce-scatter.64.cloned.1.call-update) | async-done | bytes 262160 | tf_op jit(solution)/shard_map/reduce_scatter | solution.py:437
  804.4 24.7 %reduce-scatter.66.cloned.1.call-done = f32[64,1024]{1,0:T(8,128)} async-done(((f32[256,1024]{1,0:T(8,128)}), f32[64,1024]{1,0:T(8,128)}) %reduce-scatter.66.cloned.1.call-update) | async-done | bytes 262160 | tf_op jit(solution)/shard_map/reduce_scatter | solution.py:75
  846.3 31.3 %reduce-scatter.72.cloned.1.call-done = f32[64,1024]{1,0:T(8,128)} async-done(((f32[256,1024]{1,0:T(8,128)}), f32[64,1024]{1,0:T(8,128)}) %reduce-scatter.72.cloned.1.call-update) | async-done | bytes 262160 | tf_op jit(solution)/shard_map/reduce_scatter | solution.py:437
  878.9 8.9 collective-permute-done.3
  914.0 23.7 %reduce-scatter.74.cloned.1.call-done = f32[64,1024]{1,0:T(8,128)} async-done(((f32[256,1024]{1,0:T(8,128)}), f32[64,1024]{1,0:T(8,128)}) %reduce-scatter.74.cloned.1.call-update) | async-done | bytes 262160 | tf_op jit(solution)/shard_map/reduce_scatter | solution.py:75
  961.3 10.2 reduce-scatter.60.cloned.1.call-done
  971.5 33.9 %reduce-scatter.68.cloned.1.call-done = f32[64,1024]{1,0:T(8,128)} async-done(((f32[256,1024]{1,0:T(8,128)}), f32[64,1024]{1,0:T(8,128)}) %reduce-scatter.68.cloned.1.call-update) | async-done | bytes 262160 | tf_op jit(solution)/shard_map/reduce_scatter | solution.py:436
  1005.4 33.9 %reduce-scatter.76.cloned.1.call-done = f32[64,1024]{1,0:T(8,128)} async-done(((f32[256,1024]{1,0:T(8,128)}), f32[64,1024]{1,0:T(8,128)}) %reduce-scatter.76.cloned.1.call-update) | async-done | bytes 262160 | tf_op jit(solution)/shard_map/reduce_scatter | solution.py:436
  1042.9 8.4 all_gather.154
  1057.0 9.2 all_gather.157
  1072.4 9.4 all_gather.151
  1102.8 19.3 reduce-scatter.78.cloned.1.call-done
  1122.2 33.9 %reduce-scatter.62.cloned.1.call-done = f32[64,1024]{1,0:T(8,128)} async-done(((f32[256,1024]{1,0:T(8,128)}), f32[64,1024]{1,0:T(8,128)}) %reduce-scatter.62.cloned.1.call-update) | async-done | bytes 262160 | tf_op jit(solution)/shard_map/reduce_scatter | solution.py:75
  1197.8 33.9 %reduce-scatter.88.cloned.1.call-done = f32[64,256]{1,0:T(8,128)} async-done(((f32[1024,256]{1,0:T(8,128)}), f32[64,256]{1,0:T(8,128)}) %reduce-scatter.88.cloned.1.call-update) | async-done | bytes 65552
  1234.9 72.0 %reduce-scatter.94.cloned.1.call-done = f32[64,3]{1,0:T(8,128)} async-done(((f32[1024,3]{1,0:T(8,128)}), f32[64,3]{1,0:T(8,128)}) %reduce-scatter.94.cloned.1.call-update) | async-done | bytes 784
  1307.7 73.9 %reduce-scatter.92.cloned.1.call-done = f32[64,3]{1,0:T(8,128)} async-done(((f32[1024,3]{1,0:T(8,128)}), f32[64,3]{1,0:T(8,128)}) %reduce-scatter.92.cloned.1.call-update) | async-done | bytes 784
  1391.5 70.8 %reduce-scatter.90.cloned.1.call-done = f32[64,1024]{1,0:T(8,128)} async-done(((f32[1024,1024]{1,0:T(8,128)}), f32[64,1024]{1,0:T(8,128)}) %reduce-scatter.90.cloned.1.call-update) | async-done | bytes 262160
  1464.3 161.1 %reduce-scatter.96.cloned.1.call-done = f32[32,256]{1,0:T(8,128)} async-done(((f32[1024,256]{1,0:T(8,128)}), f32[32,256]{1,0:T(8,128)}) %reduce-scatter.96.cloned.1.call-update) | async-done | bytes 32784
  1625.4 160.5 %reduce-scatter.84.cloned.1.call-done = f32[32,256]{1,0:T(8,128)} async-done(((f32[1024,256]{1,0:T(8,128)}), f32[32,256]{1,0:T(8,128)}) %reduce-scatter.84.cloned.1.call-update) | async-done | bytes 32784 | tf_op jit(solution)/shard_map/reduce_scatter | solution.py:486
  1785.9 162.8 %reduce-scatter.86.cloned.1.call-done = f32[32,512]{1,0:T(8,128)} async-done(((f32[1024,512]{1,0:T(8,128)}), f32[32,512]{1,0:T(8,128)}) %reduce-scatter.86.cloned.1.call-update) | async-done | bytes 65552 | tf_op jit(solution)/shard_map/reduce_scatter | solution.py:487
  1948.6 78.6 %reduce-scatter.82.cloned.1.call-done = f32[64,1024]{1,0:T(8,128)} async-done(((f32[1024,1024]{1,0:T(8,128)}), f32[64,1024]{1,0:T(8,128)}) %reduce-scatter.82.cloned.1.call-update) | async-done | bytes 262160 | tf_op jit(solution)/shard_map/reduce_scatter | solution.py:480
  2027.2 78.9 %reduce-scatter.80.cloned.1.call-done = f32[64,768]{1,0:T(8,128)} async-done(((f32[1024,768]{1,0:T(8,128)}), f32[64,768]{1,0:T(8,128)}) %reduce-scatter.80.cloned.1.call-update) | async-done | bytes 196624 | tf_op jit(solution)/shard_map/reduce_scatter | solution.py:478
  (942 shorter events, 334.5 us)
Async XLA Ops:
  7.2 131.4 %all-gather.5.cloned.1.call-start = ((), (), s32[]{:S(2)}) async-start(), calls=%async_computation.29 | async-start | bytes 1671168 | tf_op jit(solution)/shard_map/all_gather | solution.py:231
  7.9 310.2 %all-gather.7.cloned.1.call-start = ((), (), s32[]{:S(2)}) async-start(), calls=%async_computation.31 | async-start | bytes 1081344 | tf_op jit(solution)/shard_map/all_gather | solution.py:240
  8.7 312.0 %reduce-scatter.46.cloned.1.call-start = ((), (), s32[]{:S(2)}) async-start(), calls=%async_computation.36 | async-start | bytes 1310720 | tf_op jit(solution)/shard_map/reduce_scatter | solution.py:75
  154.9 165.7 %reduce-scatter.40.cloned.1.call-start = ((), (), s32[]{:S(2)}) async-start(), calls=%async_computation.30 | async-start | bytes 1310720 | tf_op jit(solution)/shard_map/reduce_scatter | solution.py:75
  156.4 83.4 %copy-start.193 = (bf16[256,32]{0,1:T(8,128)(2,1)S(1)}, bf16[256,32]{0,1:T(8,128)(2,1)}, u32[]{:S(2)}) copy-start(bf16[256,32]{0,1:T(8,128)(2,1)} %param.23) | copy-start | bytes 49156
  156.4 164.3 %reduce-scatter.52.cloned.1.call-start = ((), (), s32[]{:S(2)}) async-start(), calls=%async_computation.39 | async-start | bytes 1310720 | tf_op jit(solution)/shard_map/reduce_scatter | solution.py:75
  157.8 206.9 %reduce-scatter.42.cloned.1.call-start = ((), (), s32[]{:S(2)}) async-start(), calls=%async_computation.32 | async-start | bytes 1310720 | tf_op jit(solution)/shard_map/reduce_scatter | solution.py:75
  239.8 267.7 %copy-start.2 = (bf16[1024,256]{1,0:T(8,128)(2,1)}, bf16[1024,256]{1,0:T(8,128)(2,1)S(1)}, u32[]{:S(2)}) copy-start(bf16[1024,256]{1,0:T(8,128)(2,1)S(1)} %all_gather.65) | copy-start | bytes 1572868
  322.1 172.6 %copy-start.34 = (f32[64,1024]{1,0:T(8,128)}, f32[64,1024]{1,0:T(8,128)S(1)}, u32[]{:S(2)}) copy-start(f32[64,1024]{1,0:T(8,128)S(1)} %get-tuple-element.197) | copy-start | bytes 786436
  335.6 76.0 %all-gather.9.cloned.1.call-start = ((), (), s32[]{:S(2)}) async-start(), calls=%async_computation.33 | async-start | bytes 2228224 | tf_op jit(solution)/shard_map/all_gather | solution.py:233
  336.4 121.9 %all-gather.11.cloned.1.call-start = ((), (), s32[]{:S(2)}) async-start(), calls=%async_computation.34 | async-start | bytes 2228224 | tf_op jit(solution)/shard_map/all_gather | solution.py:234
  337.1 156.3 %reduce-scatter.44.cloned.1.call-start = ((), (), s32[]{:S(2)}) async-start(), calls=%async_computation.35 | async-start | bytes 1310720 | tf_op jit(solution)/shard_map/reduce_scatter | solution.py:75
  365.8 127.6 %copy-start.14 = (f32[64,1024]{1,0:T(8,128)}, f32[64,1024]{1,0:T(8,128)S(1)}, u32[]{:S(2)}) copy-start(f32[64,1024]{1,0:T(8,128)S(1)} %get-tuple-element.173) | copy-start | bytes 786436
  375.0 87.1 %copy-start.17 = (bf16[256,1024]{1,0:T(8,128)(2,1)}, bf16[256,1024]{1,0:T(8,128)(2,1)S(1)}, u32[]{:S(2)}) copy-start(bf16[256,1024]{1,0:T(8,128)(2,1)S(1)} %all_gather.67) | copy-start | bytes 1572868
  462.2 91.8 %reduce-scatter.48.cloned.1.call-start = ((), (), s32[]{:S(2)}) async-start(), calls=%async_computation.37 | async-start | bytes 1310720 | tf_op jit(solution)/shard_map/reduce_scatter | solution.py:75
  496.1 12.4 collective-permute-start
  522.2 78.8 %reduce-scatter.50.cloned.1.call-start = ((), (), s32[]{:S(2)}) async-start(), calls=%async_computation.38 | async-start | bytes 1310720 | tf_op jit(solution)/shard_map/reduce_scatter | solution.py:75
  569.6 89.3 %reduce-scatter.58.cloned.1.call-start = ((), (), s32[]{:S(2)}) async-start(), calls=%async_computation.42 | async-start | bytes 1310720 | tf_op jit(solution)/shard_map/reduce_scatter | solution.py:75
  621.2 65.2 %reduce-scatter.54.cloned.1.call-start = ((), (), s32[]{:S(2)}) async-start(), calls=%async_computation.40 | async-start | bytes 1310720 | tf_op jit(solution)/shard_map/reduce_scatter | solution.py:75
  622.8 14.5 collective-permute-start.1
  653.4 82.1 %reduce-scatter.56.cloned.1.call-start = ((), (), s32[]{:S(2)}) async-start(), calls=%async_computation.41 | async-start | bytes 1310720 | tf_op jit(solution)/shard_map/reduce_scatter | solution.py:75
  704.1 65.1 %reduce-scatter.64.cloned.1.call-start = ((), (), s32[]{:S(2)}) async-start(), calls=%async_computation.45 | async-start | bytes 1310720 | tf_op jit(solution)/shard_map/reduce_scatter | solution.py:437
  722.3 106.8 %reduce-scatter.66.cloned.1.call-start = ((), (), s32[]{:S(2)}) async-start(), calls=%async_computation.46 | async-start | bytes 1310720 | tf_op jit(solution)/shard_map/reduce_scatter | solution.py:75
  769.2 10.3 collective-permute-start.2
  797.6 80.0 %reduce-scatter.72.cloned.1.call-start = ((), (), s32[]{:S(2)}) async-start(), calls=%async_computation.49 | async-start | bytes 1310720 | tf_op jit(solution)/shard_map/reduce_scatter | solution.py:437
  846.3 91.4 %reduce-scatter.74.cloned.1.call-start = ((), (), s32[]{:S(2)}) async-start(), calls=%async_computation.50 | async-start | bytes 1310720 | tf_op jit(solution)/shard_map/reduce_scatter | solution.py:75
  877.6 10.3 collective-permute-start.3
  906.2 65.3 %reduce-scatter.60.cloned.1.call-start = ((), (), s32[]{:S(2)}) async-start(), calls=%async_computation.43 | async-start | bytes 1310720 | tf_op jit(solution)/shard_map/reduce_scatter | solution.py:436
  909.0 96.4 %reduce-scatter.68.cloned.1.call-start = ((), (), s32[]{:S(2)}) async-start(), calls=%async_computation.47 | async-start | bytes 1310720 | tf_op jit(solution)/shard_map/reduce_scatter | solution.py:436
  913.9 125.4 %reduce-scatter.76.cloned.1.call-start = ((), (), s32[]{:S(2)}) async-start(), calls=%async_computation.51 | async-start | bytes 1310720 | tf_op jit(solution)/shard_map/reduce_scatter | solution.py:436
  953.3 85.9 %copy-start.33 = (f32[64,1024]{1,0:T(8,128)S(1)}, f32[64,1024]{1,0:T(8,128)}, u32[]{:S(2)}) copy-start(f32[64,1024]{1,0:T(8,128)} %copy-done.32) | copy-start | bytes 786436
  953.3 85.9 %copy-start.35 = (f32[64,1024]{1,0:T(8,128)S(1)}, f32[64,1024]{1,0:T(8,128)}, u32[]{:S(2)}) copy-start(f32[64,1024]{1,0:T(8,128)} %copy-done.34) | copy-start | bytes 786436
  953.3 85.9 %copy-start.37 = (f32[64,1024]{1,0:T(8,128)S(1)}, f32[64,1024]{1,0:T(8,128)}, u32[]{:S(2)}) copy-start(f32[64,1024]{1,0:T(8,128)} %copy-done.36) | copy-start | bytes 786436
  953.4 149.5 %reduce-scatter.70.cloned.1.call-start = ((), (), s32[]{:S(2)}) async-start(), calls=%async_computation.48 | async-start | bytes 1310720 | tf_op jit(solution)/shard_map/reduce_scatter | solution.py:75
  955.9 96.1 %copy-start.73 = (bf16[256,768]{0,1:T(8,128)(2,1)}, bf16[256,768]{0,1:T(8,128)(2,1)S(1)}, u32[]{:S(2)}) copy-start(bf16[256,768]{0,1:T(8,128)(2,1)S(1)} %copy.397) | copy-start | bytes 1179652
  955.9 85.7 %copy-start.121 = (f32[64,1024]{1,0:T(8,128)S(1)}, f32[64,1024]{1,0:T(8,128)}, u32[]{:S(2)}) copy-start(f32[64,1024]{1,0:T(8,128)} %get-tuple-element.145) | copy-start | bytes 786436
  1056.9 65.3 %reduce-scatter.78.cloned.1.call-start = ((), (), s32[]{:S(2)}) async-start(), calls=%async_computation.52 | async-start | bytes 1310720 | tf_op jit(solution)/shard_map/reduce_scatter | solution.py:75
  1072.4 83.7 %reduce-scatter.62.cloned.1.call-start = ((), (), s32[]{:S(2)}) async-start(), calls=%async_computation.44 | async-start | bytes 1310720 | tf_op jit(solution)/shard_map/reduce_scatter | solution.py:75
  1088.1 143.6 %reduce-scatter.88.cloned.1.call-start = ((), (), s32[]{:S(2)}) async-start(), calls=%async_computation.57 | async-start | bytes 1114112
  1094.1 212.7 %reduce-scatter.94.cloned.1.call-start = ((), (), s32[]{:S(2)}) async-start(), calls=%async_computation.60 | async-start | bytes 557056
  1160.2 221.3 %reduce-scatter.92.cloned.1.call-start = ((), (), s32[]{:S(2)}) async-start(), calls=%async_computation.59 | async-start | bytes 557056
  1161.4 300.8 %reduce-scatter.90.cloned.1.call-start = ((), (), s32[]{:S(2)}) async-start(), calls=%async_computation.58 | async-start | bytes 4456448
  1173.0 452.4 %reduce-scatter.96.cloned.1.call-start = ((), (), s32[]{:S(2)}) async-start(), calls=%async_computation.61 | async-start | bytes 1081344
  1176.7 609.2 %reduce-scatter.84.cloned.1.call-start = ((), (), s32[]{:S(2)}) async-start(), calls=%async_computation.55 | async-start | bytes 1081344 | tf_op jit(solution)/shard_map/reduce_scatter | solution.py:486
  1179.5 769.1 %reduce-scatter.86.cloned.1.call-start = ((), (), s32[]{:S(2)}) async-start(), calls=%async_computation.56 | async-start | bytes 2162688 | tf_op jit(solution)/shard_map/reduce_scatter | solution.py:487
  1184.4 842.8 %reduce-scatter.82.cloned.1.call-start = ((), (), s32[]{:S(2)}) async-start(), calls=%async_computation.54 | async-start | bytes 4456448 | tf_op jit(solution)/shard_map/reduce_scatter | solution.py:480
  1190.7 915.5 %reduce-scatter.80.cloned.1.call-start = ((), (), s32[]{:S(2)}) async-start(), calls=%async_computation.53 | async-start | bytes 3342336 | tf_op jit(solution)/shard_map/reduce_scatter | solution.py:478
  1234.8 871.3 %copy-start.136 = (f32[1,2,64,1024]{3,2,1,0:T(8,128)}, f32[1,2,64,1024]{3,2,1,0:T(8,128)S(1)}, u32[]{:S(2)}) copy-start(f32[1,2,64,1024]{3,2,1,0:T(8,128)S(1)} %bitcast_dynamic-update-slice_fusion) | copy-start | bytes 1572868
  (264 other events, 2711.4 us)
Sparse Core Ops, SparseCore 0:
  10.2 46.8 all-gather.4
  58.7 150.3 all-gather.6
  211.8 32.1 reduce-scatter.45
  246.6 31.1 reduce-scatter.39
  280.4 31.2 reduce-scatter.51
  335.7 28.9 reduce-scatter.41
  366.9 44.6 all-gather.8
  413.7 44.5 all-gather.10
  462.3 31.0 reduce-scatter.43
  522.4 31.6 reduce-scatter.47
  569.7 31.2 reduce-scatter.49
  621.3 31.1 reduce-scatter.57
  655.2 31.2 reduce-scatter.53
  704.2 31.2 reduce-scatter.55
  738.0 31.2 reduce-scatter.63
  797.8 31.3 reduce-scatter.65
  846.4 31.2 reduce-scatter.71
  906.3 31.3 reduce-scatter.73
  940.3 31.1 reduce-scatter.59
  974.2 31.1 reduce-scatter.67
  1008.1 31.1 reduce-scatter.75
  1057.0 31.2 reduce-scatter.69
  1090.9 31.2 reduce-scatter.77
  1124.8 31.1 reduce-scatter.61
  1159.3 72.4 reduce-scatter.87
  1235.1 71.6 reduce-scatter.93
  1309.9 71.6 reduce-scatter.91
  1385.2 76.9 reduce-scatter.89
  1465.2 160.1 reduce-scatter.95
  1628.3 157.5 reduce-scatter.83
  1788.8 159.7 reduce-scatter.85
  1952.9 74.2 reduce-scatter.81
  2030.9 75.1 reduce-scatter.79
where the time goes:
time: 2120 us; the launch traced here: 2110 us
  waiting for transfers between devices  1390 us (66%)
  blocking collectives  415 us (20%)
  matrix products  117 us (6%)
  local copies, waits for them, and re-layouts  84.2 us (4%)
  other arithmetic  77.6 us (4%)
    unnamed x38, waiting for transfers between devices  415 us
    reduce_scatter x15, waiting for transfers between devices, sum_rows(): return lax.psum_scatter(values, 'tensor', scatter_dimension=0, tiled=True)  260 us
    all_gather x20, blocking collectives, gather_rows(): return lax.all_gather(values, 'tensor', axis=0, tiled=True)  174 us
    reduce_scatter x1, waiting for transfers between devices, shards(): lax.psum_scatter(grad_keyval, ('section', 'dp'), scatter_dimension=0, til...  163 us
    reduce_scatter x1, waiting for transfers between devices, shards(): lax.psum_scatter(grad_query, ('section', 'dp'), scatter_dimension=0, tile...  160 us
    all_gather x1, blocking collectives, fetch(): lax.all_gather(cross_query, ('section', 'dp'), axis=0, tiled=True)  81.1 us
    reduce_scatter x1, waiting for transfers between devices, shards(): lax.psum_scatter(grad_qkv, 'dp', scatter_dimension=0, tiled=True)  78.9 us
    reduce_scatter x1, waiting for transfers between devices, shards(): lax.psum_scatter(grad_up, 'dp', scatter_dimension=0, tiled=True)  78.6 us
  transfers between devices with their start and end apart: 37, of which 28 were waited for; matrix products, arithmetic and copies ran while one was open for 9% of the time, Pallas kernels for 0%

commit v1 on v0

v1 whole, which is shorter than its diff:
```python
import jax
import jax.numpy as jnp
import numpy as np
from jax import lax
from jax.sharding import Mesh
from jax.sharding import PartitionSpec as P

HEAD_DIM = 64
ROW_LEN = 256
QUARTER = 64

EPSILON = 1e-05
NEGATIVE = -1000000000.0
SCALING = 0.125
GELU_COEF = 0.7978845608028654
BFLOAT = jnp.bfloat16
FLOAT = jnp.float32
AXES = ("s", "x", "z", "h", "c")
PLANE = ("x", "z")
ORDER = np.concatenate([np.arange(QUARTER) + QUARTER * q for q in (0, 2, 1, 3)]).astype(np.int32)


def swap(block, axis):
    return lax.ppermute(block, axis, [(0, 1), (1, 0)])


def gelu_tanh(values):
    return (
        0.5 * values * (1.0 + jnp.tanh(GELU_COEF * (values + 0.044715 * values * values * values)))
    )


def layer_norm(values, gain, offset):
    centred = values - jnp.mean(values, axis=-1, keepdims=True)
    inverse = lax.rsqrt(jnp.mean(centred * centred, axis=-1, keepdims=True) + EPSILON)
    normed = centred * inverse
    return ((normed * gain + offset).astype(BFLOAT), normed, inverse)


def norm_backward(grad_out, normed, inverse, gain):
    scaled = grad_out * gain
    inner = (
        scaled
        - jnp.mean(scaled, axis=-1, keepdims=True)
        - normed * jnp.mean(scaled * normed, axis=-1, keepdims=True)
    )
    return (inverse * inner, jnp.sum(grad_out * normed, axis=0), jnp.sum(grad_out, axis=0))


def segment_ids(lengths_row):
    ends = jnp.cumsum(lengths_row)
    positions = jnp.asarray(ORDER)
    return jnp.sum((positions[:, None] >= ends[None, :]).astype(jnp.int32), axis=1)


def dot(left, right):
    return jnp.dot(left, right, preferred_element_type=FLOAT)


def dot_left(left, right):
    return lax.dot_general(left, right, (((0,), (0,)), ((), ())), preferred_element_type=FLOAT)


def dot_right(left, right):
    return lax.dot_general(left, right, (((1,), (1,)), ((), ())), preferred_element_type=FLOAT)


def attend_forward(query_heads, key_heads, value_heads, allowed):
    scores = (
        jnp.einsum("qhd,khd->hqk", query_heads, key_heads, preferred_element_type=FLOAT) * SCALING
    )
    scores = jnp.where(allowed[None], scores, NEGATIVE)
    highest = jnp.max(scores, axis=-1, keepdims=True)
    expo_scores = jnp.exp(scores - highest)
    weights = expo_scores / jnp.sum(expo_scores, axis=-1, keepdims=True)
    mixed = jnp.einsum(
        "hqk,khd->qhd", weights.astype(BFLOAT), value_heads, preferred_element_type=FLOAT
    )
    return (mixed.reshape(mixed.shape[0], -1).astype(BFLOAT), weights)


def attend_backward(query_heads, key_heads, value_heads, weights, grad_mixed):
    grad_values = jnp.einsum(
        "hqk,qhd->khd", weights.astype(BFLOAT), grad_mixed, preferred_element_type=FLOAT
    )
    grad_weights = jnp.einsum("qhd,khd->hqk", grad_mixed, value_heads, preferred_element_type=FLOAT)
    grad_scores = weights * (
        grad_weights - jnp.sum(weights * grad_weights, axis=-1, keepdims=True)
    )
    grad_scores = grad_scores.astype(BFLOAT)
    grad_queries = (
        jnp.einsum("hqk,khd->qhd", grad_scores, key_heads, preferred_element_type=FLOAT) * SCALING
    )
    grad_keys = (
        jnp.einsum("hqk,qhd->khd", grad_scores, query_heads, preferred_element_type=FLOAT) * SCALING
    )
    return (grad_queries, grad_keys, grad_values)


def gather_plane(block):
    return lax.all_gather(block, PLANE, axis=0, tiled=True)


def scatter_plane(block):
    return lax.psum_scatter(block, PLANE, scatter_dimension=0, tiled=True)


def core_sum(part):
    return part + swap(part.astype(BFLOAT), "c").astype(FLOAT)


def shards(
    embedded,
    cotangent,
    lengths,
    attn_qkv,
    attn_out,
    ffn_up,
    ffn_down,
    norm_gain,
    norm_bias,
    cross_query,
    cross_kv,
    cross_out,
):
    is_decoder = lax.axis_index("s") == 1
    first_half = lax.axis_index("h") == 0
    core = lax.axis_index("c")

    def pick(flag, yes, no):
        return jnp.where(flag, yes, no)

    def own_row(pair):
        mine = pick(first_half, pair[0], pair[1])
        got = swap(pick(first_half, pair[1], pair[0]), "h")
        half = jnp.concatenate([pick(first_half, mine, got), pick(first_half, got, mine)])
        return lax.all_gather(half, "c", axis=0, tiled=True)

    def to_owners(row):
        half = lax.dynamic_slice_in_dim(row, core * 2 * QUARTER, 2 * QUARTER, 0)
        low, high = half[:QUARTER], half[QUARTER:]
        mine = pick(first_half, low, high)
        got = swap(pick(first_half, high, low), "h")
        return jnp.stack([pick(first_half, mine, got), pick(first_half, got, mine)])

    norms = jnp.concatenate([norm_gain[0], norm_bias[0]]).T
    norms = jnp.pad(norms, ((0, 0), (0, 128 - norms.shape[1])))
    own_attn = jnp.concatenate([attn_qkv[0], attn_out[0].T], axis=1)
    own_ffn = jnp.concatenate([ffn_up[0], ffn_down[0].T], axis=1)
    query_out = jnp.concatenate([cross_query, cross_out.T], axis=1)
    kept = pick(is_decoder, query_out, cross_kv)
    got = swap(pick(is_decoder, cross_kv, query_out), "s")
    own_cross = jnp.concatenate([pick(is_decoder, got, kept), pick(is_decoder, kept, got)])
    other_attn = swap(own_attn, "h")
    other_ffn = swap(own_ffn, "h")
    other_cross = swap(own_cross, "h")
    qkv_width = attn_qkv.shape[2]
    out_width = attn_out.shape[1]
    ff_width = ffn_up.shape[2]
    cross_width = cross_kv.shape[1]
    attn_whole = gather_plane(
        jnp.concatenate(
            [
                own_attn[:, :qkv_width],
                other_attn[:, :qkv_width],
                own_attn[:, qkv_width:],
                other_attn[:, qkv_width:],
                norms,
            ],
            axis=1,
        )
    )
    ffn_whole = gather_plane(
        jnp.concatenate(
            [
                own_ffn[:, :ff_width],
                other_ffn[:, :ff_width],
                own_ffn[:, ff_width:],
                other_ffn[:, ff_width:],
            ],
            axis=1,
        )
    )
    half_cross = cross_width // 2
    key_value_pack = jnp.concatenate([own_cross, other_cross], axis=1)
    query_out_pack = jnp.concatenate(
        [
            own_cross[:, :half_cross],
            other_cross[:, :half_cross],
            own_cross[:, half_cross:],
            other_cross[:, half_cross:],
        ],
        axis=1,
    )
    cross_pack = pick(is_decoder, query_out_pack, key_value_pack)
    cross_whole = gather_plane(cross_pack)
    depth = cross_whole.shape[0]
    cross_whole = (
        cross_whole.reshape(-1, 2, cross_query.shape[0], 2 * cross_width)
        .swapaxes(0, 1)
        .reshape(depth, 2 * cross_width)
    )

    weight_qkv = attn_whole[:, : 2 * qkv_width]
    weight_out = attn_whole[:, 2 * qkv_width : 2 * qkv_width + 2 * out_width]
    norm_rows = attn_whole[:, 2 * qkv_width + 2 * out_width :][:, :6].T.astype(FLOAT)
    gains, offsets = norm_rows[:3], norm_rows[3:]
    weight_up = ffn_whole[:, : 2 * ff_width]
    weight_down = ffn_whole[:, 2 * ff_width :]
    weight_query = cross_whole[:, :cross_width]
    weight_cross = cross_whole[:, cross_width:]
    weight_keyval = cross_whole

    row_lengths = pick(first_half, lengths[:, 0, 0], lengths[:, 1, 0])
    source_pair = segment_ids(row_lengths[0])
    target_pair = segment_ids(row_lengths[1])
    own_pair = pick(is_decoder, target_pair, source_pair)
    positions = jnp.asarray(ORDER)
    ordered = (positions[None, :] <= positions[:, None]) | jnp.logical_not(is_decoder)
    allowed_self = (own_pair[:, None] == own_pair[None, :]) & ordered
    allowed_cross = target_pair[:, None] == source_pair[None, :]

    values = own_row(embedded[0]).astype(FLOAT)
    grad_out = own_row(cotangent[0]).astype(FLOAT)

    def ffn_forward(stream):
        rows, unit, inverse = layer_norm(stream, gains[2], offsets[2])
        hidden = dot(rows, weight_up)
        activated = gelu_tanh(hidden).astype(BFLOAT)
        return (stream + core_sum(dot_right(activated, weight_down)), rows, unit, inverse, hidden, activated)

    def ffn_backward(grad, unit, inverse, hidden):
        low = grad.astype(BFLOAT)
        grad_activated = dot(low, weight_down)
        grad_hidden = jax.vjp(gelu_tanh, hidden)[1](grad_activated)[0].astype(BFLOAT)
        grad_rows = core_sum(dot_right(grad_hidden, weight_up))
        into, gain, offset = norm_backward(grad_rows, unit, inverse, gains[2])
        return (grad + into, low, grad_hidden, gain, offset)

    rows_one, unit_one, inverse_one = layer_norm(values, gains[0], offsets[0])
    heads = dot(rows_one, weight_qkv).astype(BFLOAT).reshape(ROW_LEN, -1, 3, HEAD_DIM)
    mixed_one, weights_one = attend_forward(heads[:, :, 0], heads[:, :, 1], heads[:, :, 2], allowed_self)
    after_self = values + core_sum(dot_right(mixed_one, weight_out))

    encoded, rows_enc, unit_enc, inverse_enc, hidden_enc, activated_enc = ffn_forward(after_self)
    memory, unit_memory, inverse_memory = layer_norm(encoded, gains[1], offsets[1])
    keyvals = lax.ppermute(dot(memory, weight_keyval).astype(BFLOAT), "s", [(0, 1)])

    rows_two, unit_two, inverse_two = layer_norm(after_self, gains[1], offsets[1])
    queries = dot(rows_two, weight_query).astype(BFLOAT).reshape(ROW_LEN, -1, HEAD_DIM)
    pair_heads = keyvals.reshape(ROW_LEN, -1, 2, HEAD_DIM)
    keys, vals = pair_heads[:, :, 0], pair_heads[:, :, 1]
    mixed_two, weights_two = attend_forward(queries, keys, vals, allowed_cross)
    after_cross = after_self + core_sum(dot_right(mixed_two, weight_cross))
    decoded, rows_dec, unit_dec, inverse_dec, hidden_dec, activated_dec = ffn_forward(after_cross)

    outputs = to_owners(pick(is_decoder, decoded.astype(BFLOAT), memory))

    grad_cross_path, low_dec, grad_hidden_dec, gain_dec, offset_dec = ffn_backward(
        grad_out, unit_dec, inverse_dec, hidden_dec
    )
    low_cross = grad_cross_path.astype(BFLOAT)
    grad_mixed_two = dot(low_cross, weight_cross).astype(BFLOAT).reshape(ROW_LEN, -1, HEAD_DIM)
    grad_q, grad_k, grad_v = attend_backward(queries, keys, vals, weights_two, grad_mixed_two)
    grad_keyvals = jnp.stack([grad_k, grad_v], axis=2).reshape(ROW_LEN, -1).astype(BFLOAT)
    grad_keyvals = lax.ppermute(grad_keyvals, "s", [(1, 0)])
    grad_queries = grad_q.reshape(ROW_LEN, -1).astype(BFLOAT)
    into_two, gain_two, offset_two = norm_backward(
        core_sum(dot_right(grad_queries, weight_query)), unit_two, inverse_two, gains[1]
    )
    grad_self_dec = grad_cross_path + into_two

    grad_memory = grad_out + core_sum(dot_right(grad_keyvals, weight_keyval))
    grad_encoded, gain_memory, offset_memory = norm_backward(
        grad_memory, unit_memory, inverse_memory, gains[1]
    )
    grad_self_enc, low_enc, grad_hidden_enc, gain_enc, offset_enc = ffn_backward(
        grad_encoded, unit_enc, inverse_enc, hidden_enc
    )

    grad_up = dot_left(
        pick(is_decoder, rows_dec, rows_enc), pick(is_decoder, grad_hidden_dec, grad_hidden_enc)
    )
    grad_down = dot_left(
        pick(is_decoder, low_dec, low_enc), pick(is_decoder, activated_dec, activated_enc)
    )
    grad_ffn = scatter_plane(jnp.concatenate([grad_up, grad_down], axis=1).astype(BFLOAT))
    grad_cross = pick(
        is_decoder,
        jnp.concatenate([dot_left(rows_two, grad_queries), dot_left(low_cross, mixed_two)], axis=1),
        dot_left(memory, grad_keyvals),
    )
    grad_cross = grad_cross.astype(BFLOAT).reshape(2, -1, cross_query.shape[0], 2 * cross_width)
    grad_cross = scatter_plane(grad_cross.swapaxes(0, 1).reshape(depth, -1))

    grad_self = pick(is_decoder, grad_self_dec, grad_self_enc)
    low_self = grad_self.astype(BFLOAT)
    grad_mixed_one = dot(low_self, weight_out).astype(BFLOAT).reshape(ROW_LEN, -1, HEAD_DIM)
    grad_projected = jnp.stack(
        attend_backward(heads[:, :, 0], heads[:, :, 1], heads[:, :, 2], weights_one, grad_mixed_one),
        axis=2,
    )
    grad_projected = grad_projected.reshape(ROW_LEN, -1).astype(BFLOAT)
    into_one, gain_one, offset_one = norm_backward(
        core_sum(dot_right(grad_projected, weight_qkv)), unit_one, inverse_one, gains[0]
    )
    grad_embedded = to_owners(grad_self + into_one)
    norm_grads = jnp.stack(
        [
            gain_one,
            pick(is_decoder, gain_two, gain_memory),
            pick(is_decoder, gain_dec, gain_enc),
            offset_one,
            pick(is_decoder, offset_two, offset_memory),
            pick(is_decoder, offset_dec, offset_enc),
        ]
    ).T
    grad_attn = jnp.concatenate(
        [
            dot_left(rows_one, grad_projected),
            dot_left(low_self, mixed_one),
            jnp.pad(norm_grads, ((0, 0), (0, 128 - norm_grads.shape[1]))),
        ],
        axis=1,
    )
    grad_attn = scatter_plane(grad_attn.astype(BFLOAT))

    def sum_halves(pairs):
        own = jnp.concatenate([own for own, _ in pairs], axis=1)
        other = jnp.concatenate([other for _, other in pairs], axis=1)
        return own.astype(FLOAT) + swap(other, "h").astype(FLOAT)

    def halves(block, start, width):
        return (block[:, start : start + width], block[:, start + width : start + 2 * width])

    total_ffn = sum_halves([halves(grad_ffn, 0, ff_width), halves(grad_ffn, 2 * ff_width, ff_width)])
    norm_part = grad_attn[:, 2 * qkv_width + 2 * out_width :]
    total_attn = sum_halves(
        [
            halves(grad_attn, 0, qkv_width),
            halves(grad_attn, 2 * qkv_width, out_width),
            (norm_part, norm_part),
        ]
    )
    cross_pairs = [
        (pick(is_decoder, as_dec, as_enc))
        for as_dec, as_enc in zip(
            [
                jnp.concatenate([grad_cross[:, :half_cross], grad_cross[:, cross_width : cross_width + half_cross]], axis=1),
                jnp.concatenate([grad_cross[:, half_cross:cross_width], grad_cross[:, cross_width + half_cross :]], axis=1),
            ],
            halves(grad_cross, 0, cross_width),
        )
    ]
    total_cross = sum_halves([tuple(cross_pairs)])
    rows_cross = cross_query.shape[0]
    low_part, high_part = total_cross[:rows_cross], total_cross[rows_cross:]
    keep_part = pick(is_decoder, high_part, low_part)
    got_part = swap(pick(is_decoder, low_part, high_part).astype(BFLOAT), "s").astype(FLOAT)
    final_query_out = pick(is_decoder, keep_part, got_part)
    final_keyval = pick(is_decoder, got_part, keep_part)

    total_norm = total_attn[:, qkv_width + out_width :][:, :6].T
    return (
        outputs[None],
        grad_embedded[None],
        total_attn[:, :qkv_width][None],
        total_attn[:, qkv_width : qkv_width + out_width].T[None],
        total_ffn[:, :ff_width][None],
        total_ffn[:, ff_width:].T[None],
        total_norm[:3][None],
        total_norm[3:][None],
        final_query_out[:, :half_cross],
        final_keyval,
        final_query_out[:, half_cross:].T,
    )


def solution(mesh):
    fine = Mesh(mesh.devices.reshape(2, 4, 4, 2, 2), AXES)
    tokens = ("x", "z", "h", "c")
    tensor = ("h", "c")
    whole = ("s", "x", "z")
    return jax.shard_map(
        shards,
        mesh=fine,
        in_specs=(
            P("s", None, tokens, None),
            P("s", None, tokens, None),
            P(None, None, PLANE, None),
            P("s", PLANE, tensor),
            P("s", tensor, PLANE),
            P("s", PLANE, tensor),
            P("s", tensor, PLANE),
            P("s", None, PLANE),
            P("s", None, PLANE),
            P(whole, tensor),
            P(whole, tensor),
            P(tensor, whole),
        ),
        out_specs=(
            P("s", None, tokens, None),
            P("s", None, tokens, None),
            P("s", PLANE, tensor),
            P("s", tensor, PLANE),
            P("s", PLANE, tensor),
            P("s", tensor, PLANE),
            P("s", None, PLANE),
            P("s", None, PLANE),
            P(whole, tensor),
            P(whole, tensor),
            P(tensor, whole),
        ),
        check_vma=False,
    )
```

time: 2120 us -> 551 us (0.26)
  waiting for transfers between devices: 1390 us -> 339 us
  blocking collectives: 415 us -> 4.6 us
  local copies, waits for them, and re-layouts: 84.2 us -> 34.5 us
  matrix products: 117 us -> 69.5 us
  other arithmetic: 77.6 us -> 38.8 us
  starting transfers between devices: 9.45 us -> 39.8 us
    reduce_scatter x24 -> x3, waiting for transfers between devices: 881 us -> 156 us  [scatter_plane(): return lax.psum_scatter(block, PLANE, scatter_dimension=0, tiled=True)]
    unnamed x38 -> x6, waiting for transfers between devices: 415 us -> 0.1 us
    all_gather x25 -> x2, blocking collectives: 407 us -> 4.6 us  [own_row(): return lax.all_gather(half, 'c', axis=0, tiled=True)]
    dot_general x86 -> x29, matrix products: 108 us -> 60.1 us  [the longest x9 20.3 us: dot(): return jnp.dot(left, right, preferred_element_type=FLOAT)]
    all_gather x4 -> x3, waiting for transfers between devices: 80 us -> 128 us  [gather_plane(): return lax.all_gather(block, PLANE, axis=0, tiled=True)]
    ppermute x4 -> x23, waiting for transfers between devices: 15.4 us -> 54.4 us  [the longest x21 33.8 us: swap(): return lax.ppermute(block, axis, [(0, 1), (1, 0)])]
    unnamed x567 -> x167, local copies, waits for them, and re-layouts: 46.6 us -> 12.7 us
    ppermute x4 -> x23, starting transfers between devices: 7.66 us -> 39.6 us  [the longest x21 33.9 us: swap(): return lax.ppermute(block, axis, [(0, 1), (1, 0)])]
  transfers between devices with their start and end apart: 37 -> 29, of which waited for: 28 -> 20; matrix products, arithmetic and copies ran while one was open for 9% -> 20% of each run, Pallas kernels for 0% -> 0%
where the time goes in v1:
time: 551 us; the launch traced here: 542 us
  waiting for transfers between devices  339 us (62%)
  matrix products  69.5 us (13%)
  starting transfers between devices  39.8 us (7%)
  other arithmetic  38.8 us (7%)
  local copies, waits for them, and re-layouts  34.5 us (6%)
  between operations  16 us (3%)
    reduce_scatter x3, waiting for transfers between devices, scatter_plane(): return lax.psum_scatter(block, PLANE, scatter_dimension=0, tiled=True)  156 us
    all_gather x3, waiting for transfers between devices, gather_plane(): return lax.all_gather(block, PLANE, axis=0, tiled=True)  128 us
    ppermute x21, starting transfers between devices, swap(): return lax.ppermute(block, axis, [(0, 1), (1, 0)])  33.9 us
    ppermute x21, waiting for transfers between devices, swap(): return lax.ppermute(block, axis, [(0, 1), (1, 0)])  33.8 us
    dot_general x9, matrix products, dot(): return jnp.dot(left, right, preferred_element_type=FLOAT)  20.3 us
    dot_general x7, matrix products, dot_left(): lax.dot_general(left, right, (((0,), (0,)), ((), ())), preferred_element_...  16.6 us
    dot_general x9, matrix products, dot_right(): lax.dot_general(left, right, (((1,), (1,)), ((), ())), preferred_element_...  16.5 us
    ppermute x1, waiting for transfers between devices, shards(): grad_keyvals = lax.ppermute(grad_keyvals, 's', [(1, 0)])  14.6 us
  transfers between devices with their start and end apart: 29, of which 20 were waited for; matrix products, arithmetic and copies ran while one was open for 20% of the time, Pallas kernels for 0%

profile of v1, /device:TPU:0, one launch (start us, length us, event | category | flops | bytes accessed | tf_op | source)
XLA Modules:
  0.0 541.9 jit_solution(18416418958487065675)
XLA Ops:
  8.4 3.4 collective-permute-start.1
  17.8 3.3 collective-permute-start.3
  21.1 5.5 %collective-permute-done.3 = bf16[64,2048]{1,0:T(8,128)(2,1)S(1)} collective-permute-done((bf16[64,2048]{1,0:T(8,128)(2,1)S(1)}, bf16[64,2048]{1,0:T(8,128)(2,1)S(1)}, u32[]{:S(2)}, u32[]{:S(2)}) %collective-permute-start.3) | collective-permute-done | bytes 262176 | tf_op jit(solution)/shard_map/ppermute | solution.py:24
  27.6 3.3 collective-permute-start
  32.3 3.3 collective-permute-done.5
  36.8 4.6 collective-permute-done.6
  42.3 2.2 all_gather.15
  44.9 27.4 %all-gather.4.cloned.1.call-done = bf16[1024,2176]{1,0:T(8,128)(2,1)} async-done(((bf16[64,2176]{1,0:T(8,128)(2,1)}), bf16[1024,2176]{1,0:T(8,128)(2,1)}) %all-gather.4.cloned.1.call-update) | async-done | bytes 4456464 | tf_op jit(solution)/shard_map/all_gather | solution.py:101
  74.9 3.0 fusion.25
  78.2 2.1 fusion.122
  86.6 58.8 %all-gather.6.cloned.1.call-done = bf16[1024,4096]{1,0:T(8,128)(2,1)} async-done(((bf16[64,4096]{1,0:T(8,128)(2,1)}), bf16[1024,4096]{1,0:T(8,128)(2,1)}) %all-gather.6.cloned.1.call-update) | async-done | bytes 8388624 | tf_op jit(solution)/shard_map/all_gather | solution.py:101
  145.5 3.7 fusion.23
  151.7 41.4 %all-gather.8.cloned.1.call-done = bf16[1024,1024]{1,0:T(8,128)(2,1)} async-done(((bf16[64,1024]{1,0:T(8,128)(2,1)}), bf16[1024,1024]{1,0:T(8,128)(2,1)}) %all-gather.8.cloned.1.call-update) | async-done | bytes 2097168 | tf_op jit(solution)/shard_map/all_gather | solution.py:101
  199.1 4.2 collective-permute-start.7
  204.0 2.9 collective-permute-start.11
  208.3 6.1 %collective-permute-done.7 = bf16[256,1024]{1,0:T(8,128)(2,1)} collective-permute-done((bf16[256,1024]{1,0:T(8,128)(2,1)}, bf16[256,1024]{1,0:T(8,128)(2,1)}, u32[]{:S(2)}, u32[]{:S(2)}) %collective-permute-start.7) | collective-permute-done | bytes 524320 | tf_op jit(solution)/shard_map/ppermute | solution.py:247
  215.6 3.1 fusion.125
  218.7 2.0 convolution_convert_fusion.9
  221.6 2.4 all_gather.19
  224.5 3.7 fusion.21
  229.5 2.9 fusion.35
  239.1 2.3 fusion.52
  245.3 14.6 %collective-permute-done.14 = bf16[256,1024]{0,1:T(8,128)(2,1)S(1)} collective-permute-done((bf16[256,1024]{0,1:T(8,128)(2,1)S(1)}, bf16[256,1024]{0,1:T(8,128)(2,1)S(1)}, u32[]{:S(2)}, u32[]{:S(2)}) %collective-permute-start.14) | collective-permute-done | bytes 524320 | tf_op jit(solution)/shard_map/ppermute | solution.py:266
  266.1 2.9 fusion.31
  269.0 2.5 fusion.131
  272.5 2.0 fusion.4
  274.6 3.9 copy.169
  278.5 3.2 copy.170
  281.8 2.9 multiply_reduce_fusion.5
  284.8 2.0 add_select_fusion
  289.7 2.2 multiply_reduce_fusion
  298.0 2.9 convolution_convert_fusion
  302.9 3.8 fusion.3
  306.9 5.0 convolution_convert_fusion.2
  311.9 4.1 convolution_convert_fusion.1
  316.0 7.8 %pad_maximum_fusion = bf16[1024,4096]{1,0:T(8,128)(2,1)} fusion(bf16[1024,2048]{1,0:T(8,128)(2,1)} %convolution_convert_fusion.1, bf16[1024,2048]{1,0:T(8,128)(2,1)} %convolution_convert_fusion.2), kind=kLoop, calls=%fused_computation.4 | loop fusion | flops 16777216 | bytes 16777216 | tf_op jit(solution)/shard_map/concatenate | solution.py:287
  323.9 5.5 %fusion.127 = (bf16[256,1024]{1,0:T(8,128)(2,1)}, f32[256,1024]{1,0:T(8,128)}) fusion(bf16[1024,4096]{1,0:T(8,128)(2,1)} %all-gather.6.cloned.1.call-done, f32[256,2048]{1,0:T(8,128)} %copy-done.72), kind=kOutput, calls=%fused_computation.305 | convolution fusion | flops 1078722560 | bytes 7864320 | tf_op jit(solution)/shard_map/dot_general | solution.py:65
  332.8 2.9 collective-permute-start.10
  335.8 4.4 collective-permute-done.10
  342.5 2.9 collective-permute-start.18
  345.4 9.9 %reduce-scatter.8.cloned.1.call-done = bf16[64,1024]{1,0:T(8,128)(2,1)} async-done(((bf16[1024,1024]{1,0:T(8,128)(2,1)}), bf16[64,1024]{1,0:T(8,128)(2,1)}) %reduce-scatter.8.cloned.1.call-update) | async-done | bytes 131088 | tf_op jit(solution)/shard_map/reduce_scatter | solution.py:105
  357.0 3.1 collective-permute-start.21
  360.1 2.7 collective-permute-done.21
  368.4 67.9 %reduce-scatter.4.cloned.1.call-done = bf16[64,2176]{1,0:T(8,128)(2,1)} async-done(((bf16[1024,2176]{1,0:T(8,128)(2,1)}), bf16[64,2176]{1,0:T(8,128)(2,1)}) %reduce-scatter.4.cloned.1.call-update) | async-done | bytes 278544 | tf_op jit(solution)/shard_map/reduce_scatter | solution.py:105
  438.1 3.1 collective-permute-start.19
  445.5 78.7 %reduce-scatter.6.cloned.1.call-done = bf16[64,4096]{1,0:T(8,128)(2,1)} async-done(((bf16[1024,4096]{1,0:T(8,128)(2,1)}), bf16[64,4096]{1,0:T(8,128)(2,1)}) %reduce-scatter.6.cloned.1.call-update) | async-done | bytes 524304 | tf_op jit(solution)/shard_map/reduce_scatter | solution.py:105
  525.3 3.1 collective-permute-start.20
  530.5 3.2 collective-permute-done.20
  (342 shorter events, 87.1 us)
Async XLA Ops:
  7.2 19.5 %copy-start.37 = (bf16[1,1024,64]{1,2,0:T(8,128)(2,1)S(1)}, bf16[1,1024,64]{1,2,0:T(8,128)(2,1)}, u32[]{:S(2)}) copy-start(bf16[1,1024,64]{1,2,0:T(8,128)(2,1)} %param.19) | copy-start | bytes 393220
  7.2 19.5 %copy-start.38 = (bf16[1,64,1024]{2,1,0:T(8,128)(2,1)S(1)}, bf16[1,64,1024]{2,1,0:T(8,128)(2,1)}, u32[]{:S(2)}) copy-start(bf16[1,64,1024]{2,1,0:T(8,128)(2,1)} %param.18) | copy-start | bytes 393220
  7.2 20.4 %copy-start.26 = (bf16[1,2,64,1024]{3,2,1,0:T(8,128)(2,1)S(1)}, bf16[1,2,64,1024]{3,2,1,0:T(8,128)(2,1)}, u32[]{:S(2)}) copy-start(bf16[1,2,64,1024]{3,2,1,0:T(8,128)(2,1)} %param.13) | copy-start | bytes 786436
  7.2 23.7 %copy-start.41 = (bf16[32,512]{1,0:T(8,128)(2,1)S(1)}, bf16[32,512]{1,0:T(8,128)(2,1)}, u32[]{:S(2)}) copy-start(bf16[32,512]{1,0:T(8,128)(2,1)} %param.23) | copy-start | bytes 98308
  7.2 23.7 %copy-start.42 = (bf16[256,32]{0,1:T(8,128)(2,1)S(1)}, bf16[256,32]{0,1:T(8,128)(2,1)}, u32[]{:S(2)}) copy-start(bf16[256,32]{0,1:T(8,128)(2,1)} %param.24) | copy-start | bytes 49156
  7.2 23.7 %copy-start.43 = (bf16[32,256]{1,0:T(8,128)(2,1)S(1)}, bf16[32,256]{1,0:T(8,128)(2,1)}, u32[]{:S(2)}) copy-start(bf16[32,256]{1,0:T(8,128)(2,1)} %param.22) | copy-start | bytes 49156
  7.2 65.1 %all-gather.4.cloned.1.call-start = ((), (), s32[]{:S(2)}) async-start(), calls=%async_computation.3 | async-start | bytes 4734976 | tf_op jit(solution)/shard_map/all_gather | solution.py:101
  7.3 24.4 %copy-start.67 = (s32[2,2,1,8]{3,2,1,0:T(1,128)S(1)}, s32[2,2,1,8]{3,2,1,0:T(1,128)}, u32[]{:S(2)}) copy-start(s32[2,2,1,8]{3,2,1,0:T(1,128)} %param.15) | copy-start | bytes 388
  7.3 24.8 %copy-start.60 = (s32[256]{0:T(256)S(1)}, s32[256]{0:T(256)}, u32[]{:S(2)}) copy-start(s32[256]{0:T(256)} %constant.69.clone) | copy-start | bytes 3076
  8.4 6.9 %collective-permute-start.1 = (bf16[64,1024]{1,0:T(8,128)(2,1)S(1)}, bf16[64,1024]{1,0:T(8,128)(2,1)S(1)}, u32[]{:S(2)}, u32[]{:S(2)}) collective-permute-start(bf16[64,1024]{1,0:T(8,128)(2,1)S(1)} %pad_maximum_fusion.9), channel_id=1, source_target_pairs={{0,2},{2,0},{1,3},{3,1},{4,6},{6,4},{5,7},{7,5},{8,10},{10,8},{9,1... | collective-permute-start | bytes 393224 | tf_op jit(solution)/shard_map/ppermute | solution.py:24
  16.8 128.7 %all-gather.6.cloned.1.call-start = ((), (), s32[]{:S(2)}) async-start(), calls=%async_computation.4 | async-start | bytes 8912896 | tf_op jit(solution)/shard_map/all_gather | solution.py:101
  17.8 8.8 %collective-permute-start.3 = (bf16[64,2048]{1,0:T(8,128)(2,1)S(1)}, bf16[64,2048]{1,0:T(8,128)(2,1)S(1)}, u32[]{:S(2)}, u32[]{:S(2)}) collective-permute-start(bf16[64,2048]{1,0:T(8,128)(2,1)S(1)} %pad_maximum_fusion.5), channel_id=1, source_target_pairs={{0,2},{2,0},{1,3},{3,1},{4,6},{6,4},{5,7},{7,5},{8,10},{10,8},{9,1... | collective-permute-start | bytes 786440 | tf_op jit(solution)/shard_map/ppermute | solution.py:24
  27.5 165.6 %all-gather.8.cloned.1.call-start = ((), (), s32[]{:S(2)}) async-start(), calls=%async_computation.5 | async-start | bytes 2228224 | tf_op jit(solution)/shard_map/all_gather | solution.py:101
  27.6 14.6 %collective-permute-start = (bf16[64,1024]{1,0:T(8,128)(2,1)S(1)}, bf16[64,1024]{1,0:T(8,128)(2,1)S(1)}, u32[]{:S(2)}, u32[]{:S(2)}) collective-permute-start(bf16[64,1024]{1,0:T(8,128)(2,1)S(1)} %select_bitcast_fusion.5), channel_id=1, source_target_pairs={{0,2},{2,0},{1,3},{3,1},{4,6},{6,4},{5,7},{7,5},{8,10},{10,8},{9,1... | collective-permute-start | bytes 393224 | tf_op jit(solution)/shard_map/ppermute | solution.py:24
  30.9 4.6 collective-permute-start.5
  35.6 5.8 %collective-permute-start.6 = (bf16[64,512]{1,0:T(8,128)(2,1)S(1)}, bf16[64,512]{1,0:T(8,128)(2,1)S(1)}, u32[]{:S(2)}, u32[]{:S(2)}) collective-permute-start(bf16[64,512]{1,0:T(8,128)(2,1)S(1)} %pad_maximum_fusion.10), channel_id=1, source_target_pairs={{0,2},{2,0},{1,3},{3,1},{4,6},{6,4},{5,7},{7,5},{8,10},{10,8},{9,1... | collective-permute-start | bytes 196616 | tf_op jit(solution)/shard_map/ppermute | solution.py:24
  42.2 313.1 %reduce-scatter.8.cloned.1.call-start = ((), (), s32[]{:S(2)}) async-start(), calls=%async_computation.8 | async-start | bytes 2228224 | tf_op jit(solution)/shard_map/reduce_scatter | solution.py:105
  44.5 41.6 %copy-start.3 = (bf16[256,1024]{1,0:T(8,128)(2,1)}, bf16[256,1024]{1,0:T(8,128)(2,1)S(1)}, u32[]{:S(2)}) copy-start(bf16[256,1024]{1,0:T(8,128)(2,1)S(1)} %all_gather.15) | copy-start | bytes 1572868
  44.6 30.3 %copy-start.58 = (f32[256]{0:T(256)}, f32[256]{0:T(256)S(1)}, u32[]{:S(2)}) copy-start(f32[256]{0:T(256)S(1)} %broadcast_multiply_fusion.14) | copy-start | bytes 3076
  44.9 33.0 %copy-start.61 = (f32[256]{0:T(256)}, f32[256]{0:T(256)S(1)}, u32[]{:S(2)}) copy-start(f32[256]{0:T(256)S(1)} %add_rsqrt_fusion.3) | copy-start | bytes 3076
  74.9 122.4 %copy-start.44 = (f32[1024]{0:T(1024)}, f32[1024]{0:T(1024)S(1)}, u32[]{:S(2)}) copy-start(f32[1024]{0:T(1024)S(1)} %get-tuple-element.91) | copy-start | bytes 12292
  84.1 2.0 collective-permute-start.2
  86.6 62.6 %copy-start.49 = (f32[256]{0:T(256)}, f32[256]{0:T(256)S(1)}, u32[]{:S(2)}) copy-start(f32[256]{0:T(256)S(1)} %add_rsqrt_fusion.2) | copy-start | bytes 3076
  151.6 43.2 %collective-permute-start.4 = (bf16[256,1024]{1,0:T(8,128)(2,1)S(1)}, bf16[256,1024]{1,0:T(8,128)(2,1)S(1)}, u32[]{:S(2)}, u32[]{:S(2)}) collective-permute-start(bf16[256,1024]{1,0:T(8,128)(2,1)S(1)} %get-tuple-element.150), channel_id=1, source_target_pairs={{0,1},{1,0},{2,3},{3,2},{4,5},{5,4},{6,7},{7,6},{8,9},{9,8},{10,11... | collective-permute-start | bytes 1572872 | tf_op jit(solution)/shard_map/ppermute | solution.py:24
  194.8 12.8 %copy-start = (bf16[2,16,32,1024]{3,2,1,0:T(8,128)(2,1)}, bf16[2,16,32,1024]{3,2,1,0:T(8,128)(2,1)S(1)}, u32[]{:S(2)}) copy-start(bf16[2,16,32,1024]{3,2,1,0:T(8,128)(2,1)S(1)} %copy.150) | copy-start | bytes 6291460
  197.5 10.6 %copy-start.21 = (bf16[256,1024]{1,0:T(8,128)(2,1)}, bf16[256,1024]{1,0:T(8,128)(2,1)S(1)}, u32[]{:S(2)}) copy-start(bf16[256,1024]{1,0:T(8,128)(2,1)S(1)} %add_convert_fusion.2) | copy-start | bytes 1572868
  199.1 15.2 %collective-permute-start.7 = (bf16[256,1024]{1,0:T(8,128)(2,1)}, bf16[256,1024]{1,0:T(8,128)(2,1)}, u32[]{:S(2)}, u32[]{:S(2)}) collective-permute-start(bf16[256,1024]{1,0:T(8,128)(2,1)} %convolution_convert_fusion.4), channel_id=1, source_target_pairs={{0,64},{1,65},{2,66},{3,67},{4,68},{5,69},{6,70},{7,71},{8,72},{9,... | collective-permute-start | bytes 1572872 | tf_op jit(solution)/shard_map/ppermute | solution.py:247
  204.0 17.5 %collective-permute-start.11 = (bf16[64,1024]{1,0:T(8,128)(2,1)}, bf16[64,1024]{1,0:T(8,128)(2,1)S(1)}, u32[]{:S(2)}, u32[]{:S(2)}) collective-permute-start(bf16[64,1024]{1,0:T(8,128)(2,1)} %select_bitcast_fusion.2), channel_id=1, source_target_pairs={{0,2},{2,0},{1,3},{3,1},{4,6},{6,4},{5,7},{7,5},{8,10},{10,8},{9,1... | collective-permute-start | bytes 393224 | tf_op jit(solution)/shard_map/ppermute | solution.py:24
  208.2 10.4 %copy-start.28 = (bf16[256,512]{0,1:T(8,128)(2,1)}, bf16[256,512]{0,1:T(8,128)(2,1)S(1)}, u32[]{:S(2)}) copy-start(bf16[256,512]{0,1:T(8,128)(2,1)S(1)} %copy.153) | copy-start | bytes 786436
  221.4 2.6 collective-permute-start.8
  224.0 12.3 %copy-start.10 = (bf16[256,1024]{1,0:T(8,128)(2,1)}, bf16[256,1024]{1,0:T(8,128)(2,1)S(1)}, u32[]{:S(2)}) copy-start(bf16[256,1024]{1,0:T(8,128)(2,1)S(1)} %all_gather.19) | copy-start | bytes 1572868
  233.7 2.0 collective-permute-start.12
  243.5 16.4 %copy-start.2 = (bf16[2,16,32,1024]{3,2,1,0:T(8,128)(2,1)S(1)}, bf16[2,16,32,1024]{3,2,1,0:T(8,128)(2,1)}, u32[]{:S(2)}) copy-start(bf16[2,16,32,1024]{3,2,1,0:T(8,128)(2,1)} %copy-done) | copy-start | bytes 6291460
  243.6 16.3 %collective-permute-start.14 = (bf16[256,1024]{0,1:T(8,128)(2,1)S(1)}, bf16[256,1024]{0,1:T(8,128)(2,1)S(1)}, u32[]{:S(2)}, u32[]{:S(2)}) collective-permute-start(bf16[256,1024]{0,1:T(8,128)(2,1)S(1)} %bitcast.226), channel_id=1, source_target_pairs={{64,0},{65,1},{66,2},{67,3},{68,4},{69,5},{70,6},{71,7},{72,8},{73... | collective-permute-start | bytes 1572872 | tf_op jit(solution)/shard_map/ppermute | solution.py:266
  245.0 19.8 %slice-start.4 = ((s8[8388608]{0:T(1024)(128)(4,1)}), s8[4194304]{0:T(1024)(128)(4,1)S(1)}, s32[]{:S(2)}) async-start(s8[8388608]{0:T(1024)(128)(4,1)} %bitcast.245), calls=%async_computation.13 | async-start | bytes 8388608
  260.7 3.0 collective-permute-start.15
  262.5 19.3 %collective-permute-start.13 = (bf16[256,1024]{1,0:T(8,128)(2,1)}, bf16[256,1024]{1,0:T(8,128)(2,1)}, u32[]{:S(2)}, u32[]{:S(2)}) collective-permute-start(bf16[256,1024]{1,0:T(8,128)(2,1)} %get-tuple-element.164), channel_id=1, source_target_pairs={{0,1},{1,0},{2,3},{3,2},{4,5},{5,4},{6,7},{7,6},{8,9},{9,8},{10,11... | collective-permute-start | bytes 1572872 | tf_op jit(solution)/shard_map/ppermute | solution.py:24
  271.5 10.3 %collective-permute-start.16 = (bf16[256,1024]{1,0:T(8,128)(2,1)}, bf16[256,1024]{1,0:T(8,128)(2,1)}, u32[]{:S(2)}, u32[]{:S(2)}) collective-permute-start(bf16[256,1024]{1,0:T(8,128)(2,1)} %get-tuple-element.166), channel_id=1, source_target_pairs={{0,1},{1,0},{2,3},{3,2},{4,5},{5,4},{6,7},{7,6},{8,9},{9,8},{10,11... | collective-permute-start | bytes 1572872 | tf_op jit(solution)/shard_map/ppermute | solution.py:24
  281.7 154.6 %reduce-scatter.4.cloned.1.call-start = ((), (), s32[]{:S(2)}) async-start(), calls=%async_computation.6 | async-start | bytes 4734976 | tf_op jit(solution)/shard_map/reduce_scatter | solution.py:105
  295.9 5.0 collective-permute-start.17
  306.8 217.4 %reduce-scatter.6.cloned.1.call-start = ((), (), s32[]{:S(2)}) async-start(), calls=%async_computation.7 | async-start | bytes 8912896 | tf_op jit(solution)/shard_map/reduce_scatter | solution.py:105
  329.5 2.2 collective-permute-start.9
  332.8 7.4 %collective-permute-start.10 = (bf16[64,1024]{1,0:T(8,128)(2,1)S(1)}, bf16[64,1024]{1,0:T(8,128)(2,1)S(1)}, u32[]{:S(2)}, u32[]{:S(2)}) collective-permute-start(bf16[64,1024]{1,0:T(8,128)(2,1)S(1)} %broadcast_select_fusion.2), channel_id=1, source_target_pairs={{0,2},{2,0},{1,3},{3,1},{4,6},{6,4},{5,7},{7,5},{8,10},{10,8},{9,1... | collective-permute-start | bytes 393224 | tf_op jit(solution)/shard_map/ppermute | solution.py:24
  342.5 17.5 %collective-permute-start.18 = (f32[64,1024]{1,0:T(8,128)S(1)}, f32[64,1024]{1,0:T(8,128)S(1)}, u32[]{:S(2)}, u32[]{:S(2)}) collective-permute-start(f32[64,1024]{1,0:T(8,128)S(1)} %slice_select_fusion), channel_id=1, source_target_pairs={{0,2},{2,0},{1,3},{3,1},{4,6},{6,4},{5,7},{7,5},{8,10},{10,8},{9,1... | collective-permute-start | bytes 786440 | tf_op jit(solution)/shard_map/ppermute | solution.py:24
  357.0 5.8 %collective-permute-start.21 = (bf16[64,512]{1,0:T(8,128)(2,1)S(1)}, bf16[64,512]{1,0:T(8,128)(2,1)S(1)}, u32[]{:S(2)}, u32[]{:S(2)}) collective-permute-start(bf16[64,512]{1,0:T(8,128)(2,1)S(1)} %slice_select_fusion.2), channel_id=1, source_target_pairs={{0,2},{2,0},{1,3},{3,1},{4,6},{6,4},{5,7},{7,5},{8,10},{10,8},{9,1... | collective-permute-start | bytes 196616 | tf_op jit(solution)/shard_map/ppermute | solution.py:24
  363.7 4.0 collective-permute-start.22
  438.1 6.7 %collective-permute-start.19 = (bf16[64,1152]{1,0:T(8,128)(2,1)S(1)}, bf16[64,1152]{1,0:T(8,128)(2,1)S(1)}, u32[]{:S(2)}, u32[]{:S(2)}) collective-permute-start(bf16[64,1152]{1,0:T(8,128)(2,1)S(1)} %pad_maximum_fusion.8), channel_id=1, source_target_pairs={{0,2},{2,0},{1,3},{3,1},{4,6},{6,4},{5,7},{7,5},{8,10},{10,8},{9,1... | collective-permute-start | bytes 442376 | tf_op jit(solution)/shard_map/ppermute | solution.py:24
  525.3 8.4 %collective-permute-start.20 = (bf16[64,2048]{1,0:T(8,128)(2,1)S(1)}, bf16[64,2048]{1,0:T(8,128)(2,1)S(1)}, u32[]{:S(2)}, u32[]{:S(2)}) collective-permute-start(bf16[64,2048]{1,0:T(8,128)(2,1)S(1)} %pad_maximum_fusion.7), channel_id=1, source_target_pairs={{0,2},{2,0},{1,3},{3,1},{4,6},{6,4},{5,7},{7,5},{8,10},{10,8},{9,1... | collective-permute-start | bytes 786440 | tf_op jit(solution)/shard_map/ppermute | solution.py:24
  (61 other events, 181.3 us)
Sparse Core Ops, SparseCore 0:
  16.9 55.3 all-gather.3
  75.0 70.4 all-gather.5
  148.2 44.8 all-gather.7
  281.8 73.4 reduce-scatter.7
  358.9 77.3 reduce-scatter.3
  439.9 84.1 reduce-scatter.5

commit v2 on v1

v2 whole, which is shorter than its diff:
```python
import functools

import jax
import jax.numpy as jnp
import numpy as np
from jax import lax
from jax.experimental import pallas as pl
from jax.experimental.pallas import tpu as pltpu
from jax.sharding import Mesh
from jax.sharding import PartitionSpec as P

HEAD_DIM = 64
ROW_LEN = 256
QUARTER = 64

EPSILON = 1e-05
NEGATIVE = -1000000000.0
SCALING = 0.125
GELU_COEF = 0.7978845608028654
BFLOAT = jnp.bfloat16
FLOAT = jnp.float32
AXES = ("s", "x", "z", "h", "c")
PLANE = ("x", "z")
ORDER = np.concatenate([np.arange(QUARTER) + QUARTER * q for q in (0, 2, 1, 3)]).astype(np.int32)


def swap(block, axis):
    return lax.ppermute(block, axis, [(0, 1), (1, 0)])


def shift(block, axis, distance):
    size = lax.axis_size(axis)
    return lax.ppermute(block, axis, [(i, (i + distance) % size) for i in range(size)])


def place(buffer, block, index, dim):
    return lax.dynamic_update_slice_in_dim(buffer, jnp.expand_dims(block, dim), index, dim)


def take(buffer, index, dim):
    return lax.dynamic_index_in_dim(buffer, index, dim, keepdims=False)


def gather_direct(block, axis):
    here = lax.axis_index(axis)
    blocks = [block, shift(block, axis, -1), shift(block, axis, 2), shift(block, axis, 1)]
    return [((here + k) % 4, block) for k, block in enumerate(blocks)]


def gather_ring(block, axis):
    here = lax.axis_index(axis)
    half = block.shape[0] // 2
    before, after = shift(block, axis, 1), shift(block, axis, -1)
    far = jnp.concatenate([shift(before[:half], axis, 1), shift(after[half:], axis, -1)])
    return [((here + k) % 4, block) for k, block in enumerate([block, after, far, before])]


def gather_ring_plane(block, axes):
    near, far = axes
    rows, columns = block.shape
    first = jnp.zeros((4, rows, columns), block.dtype)
    for index, piece in gather_direct(block, near):
        first = place(first, piece, index, 0)
    whole = jnp.zeros((4, 4, rows, columns), block.dtype)
    dim = PLANE.index(far)
    for index, piece in gather_ring(first, far):
        whole = place(whole, piece, index, dim)
    return whole.reshape(-1, columns)


def scatter_direct(blocks, axis):
    here = lax.axis_index(axis)
    parts = [take(blocks, (here + k) % 4, 0) for k in range(4)]
    total = parts[0].astype(FLOAT)
    for distance in (1, 2, -1):
        total = total + shift(parts[distance % 4].astype(BFLOAT), axis, distance).astype(FLOAT)
    return total


def scatter_ring(blocks, axis, dim):
    here = lax.axis_index(axis)
    own, after, far, before = [take(blocks, (here + k) % 4, dim) for k in range(4)]
    half = own.shape[0] // 2
    far = far.astype(BFLOAT)
    top = shift(far[:half], axis, 1).astype(FLOAT)
    bottom = shift(far[half:], axis, -1).astype(FLOAT)
    after = jnp.concatenate([after[:half].astype(FLOAT) + top, after[half:].astype(FLOAT)])
    before = jnp.concatenate([before[:half].astype(FLOAT), before[half:].astype(FLOAT) + bottom])
    from_before = shift(after.astype(BFLOAT), axis, 1).astype(FLOAT)
    from_after = shift(before.astype(BFLOAT), axis, -1).astype(FLOAT)
    return own.astype(FLOAT) + from_before + from_after


def scatter_ring_plane(block, axes):
    near, far = axes
    rows = block.shape[0] // 16
    blocks = block.reshape(4, 4, rows, -1)
    return scatter_direct(scatter_ring(blocks, far, PLANE.index(far)), near)


def gelu_tanh(values):
    return (
        0.5 * values * (1.0 + jnp.tanh(GELU_COEF * (values + 0.044715 * values * values * values)))
    )


def gelu_slope(values):
    squares = values * values
    curve = jnp.tanh(GELU_COEF * (values + 0.044715 * values * squares))
    return 0.5 * (1.0 + curve) + 0.5 * values * (1.0 - curve * curve) * (
        GELU_COEF * (1.0 + 3.0 * 0.044715 * squares)
    )


def segment_ids(lengths_row):
    ends = jnp.cumsum(lengths_row)
    positions = jnp.asarray(ORDER)
    return jnp.sum((positions[:, None] >= ends[None, :]).astype(jnp.int32), axis=1)


def dot(left, right):
    return jnp.dot(left, right, preferred_element_type=FLOAT)


def dot_left(left, right):
    return lax.dot_general(left, right, (((0,), (0,)), ((), ())), preferred_element_type=FLOAT)


def dot_right(left, right):
    return lax.dot_general(left, right, (((1,), (1,)), ((), ())), preferred_element_type=FLOAT)


def normalize(stream):
    centred = stream - jnp.mean(stream, axis=-1, keepdims=True)
    inverse = lax.rsqrt(jnp.mean(centred * centred, axis=-1, keepdims=True) + EPSILON)
    return centred * inverse, inverse


def layer_norm(stream, norms, index):
    unit, _ = normalize(stream)
    return (unit * norms[index : index + 1] + norms[index + 3 : index + 4]).astype(BFLOAT)


def norm_backward(grad_out, stream, gain):
    unit, inverse = normalize(stream)
    scaled = grad_out * gain
    inner = (
        scaled
        - jnp.mean(scaled, axis=-1, keepdims=True)
        - unit * jnp.mean(scaled * unit, axis=-1, keepdims=True)
    )
    sums = jnp.concatenate(
        [
            jnp.sum(grad_out * unit, axis=0, keepdims=True),
            jnp.sum(grad_out, axis=0, keepdims=True),
            jnp.zeros((6, grad_out.shape[1]), FLOAT),
        ]
    )
    return inverse * inner, sums


def add_parts(own_ref, other_ref):
    return own_ref[...].astype(FLOAT) + other_ref[...].astype(FLOAT)


def softmax(query, key, mask):
    scores = jnp.where(mask, dot_right(query, key) * SCALING, NEGATIVE)
    expo_scores = jnp.exp(scores - jnp.max(scores, axis=-1, keepdims=True))
    return expo_scores / jnp.sum(expo_scores, axis=-1, keepdims=True)


def head_backward(query, key, value, mask, grad_mixed):
    weights = softmax(query, key, mask)
    grad_value = dot_left(weights.astype(BFLOAT), grad_mixed)
    grad_weights = dot_right(grad_mixed, value)
    grad_scores = weights * (
        grad_weights - jnp.sum(weights * grad_weights, axis=-1, keepdims=True)
    )
    grad_scores = grad_scores.astype(BFLOAT)
    grad_query = dot(grad_scores, key) * SCALING
    grad_key = dot_left(grad_scores, query) * SCALING
    return grad_query.astype(BFLOAT), grad_key.astype(BFLOAT), grad_value.astype(BFLOAT)


def head(ref, place):
    return ref[:, place * HEAD_DIM : (place + 1) * HEAD_DIM]


def self_forward_kernel(stream, norms, own, other, mask, rows, qkv, mixed, part):
    allowed = mask[...] > 0.5
    normed = layer_norm(stream[...], norms, 0)
    rows[...] = normed
    quarter = mixed.shape[1] // 2
    width = 3 * quarter
    total = None
    for side, weights in enumerate((own, other)):
        qkv[:, side * width : (side + 1) * width] = dot(normed, weights[:, :width]).astype(BFLOAT)
        first = side * quarter // HEAD_DIM
        for i in range(first, first + quarter // HEAD_DIM):
            weight = softmax(head(qkv, 3 * i), head(qkv, 3 * i + 1), allowed)
            out = dot(weight.astype(BFLOAT), head(qkv, 3 * i + 2))
            mixed[:, i * HEAD_DIM : (i + 1) * HEAD_DIM] = out.astype(BFLOAT)
        term = dot_right(
            mixed[:, side * quarter : (side + 1) * quarter], weights[:, width : width + quarter]
        )
        total = term if total is None else total + term
    part[...] = total.astype(BFLOAT)


def ffn_forward_kernel(
    stream, own, other, norms, up, down, after, rows, hidden, activated, part, total
):
    step = pl.program_id(0)

    @pl.when(step == 0)
    def _():
        after[...] = stream[...] + add_parts(own, other)
        rows[...] = layer_norm(after[...], norms, 2)

    raised = dot(rows[...], up[...])
    hidden[...] = raised
    active = gelu_tanh(raised).astype(BFLOAT)
    activated[...] = active
    term = dot_right(active, down[...])

    @pl.when(step == 0)
    def _():
        total[...] = term

    @pl.when(step > 0)
    def _():
        total[...] += term

    @pl.when(step == pl.num_programs(0) - 1)
    def _():
        part[...] = total[...].astype(BFLOAT)


def memory_kernel(stream, own, other, norms, weights, encoded, memory, keyvals):
    encoded[...] = stream[...] + add_parts(own, other)
    memory[...] = layer_norm(encoded[...], norms, 1)
    keyvals[...] = dot(memory[...], weights[...]).astype(BFLOAT)


def query_kernel(stream, own, other, norms, weights, after, rows, queries):
    after[...] = stream[...] + add_parts(own, other)
    rows[...] = layer_norm(after[...], norms, 1)
    queries[...] = dot(rows[...], weights[:, : queries.shape[1]]).astype(BFLOAT)


def cross_forward_kernel(queries, keyvals, mask, weights, mixed, part):
    allowed = mask[...] > 0.5
    for i in range(queries.shape[1] // HEAD_DIM):
        weight = softmax(head(queries, i), head(keyvals, 2 * i), allowed)
        out = dot(weight.astype(BFLOAT), head(keyvals, 2 * i + 1))
        mixed[:, i * HEAD_DIM : (i + 1) * HEAD_DIM] = out.astype(BFLOAT)
    part[...] = dot_right(mixed[...], weights[:, queries.shape[1] :]).astype(BFLOAT)


def ffn_backward_step(low, hidden, up, down, grad_hidden, part, total):
    step = pl.program_id(0)
    grad_activated = dot(low[...], down[...])
    grad = (grad_activated * gelu_slope(hidden[...])).astype(BFLOAT)
    grad_hidden[...] = grad
    term = dot_right(grad, up[...])

    @pl.when(step == 0)
    def _():
        total[...] = term

    @pl.when(step > 0)
    def _():
        total[...] += term

    @pl.when(step == pl.num_programs(0) - 1)
    def _():
        part[...] = total[...].astype(BFLOAT)


def ffn_backward_kernel(low, hidden, up, down, grad_hidden, part, total):
    ffn_backward_step(low, hidden, up, down, grad_hidden, part, total)


def memory_ffn_backward_kernel(
    cotangent, own, other, stream, norms, hidden, up, down, grad, low, sums, grad_hidden, part, total
):
    @pl.when(pl.program_id(0) == 0)
    def _():
        into, totals = norm_backward(
            cotangent[...].astype(FLOAT) + add_parts(own, other), stream[...], norms[1:2]
        )
        grad[...] = into
        low[...] = into.astype(BFLOAT)
        sums[...] = totals

    ffn_backward_step(low, hidden, up, down, grad_hidden, part, total)


def cross_backward_kernel(
    cotangent, own, other, stream, norms, queries, keyvals, mask, weights,
    grad, low, sums, grad_queries, grad_keyvals, part,
):
    allowed = mask[...] > 0.5
    into, totals = norm_backward(add_parts(own, other), stream[...], norms[2:3])
    grad[...] = cotangent[...].astype(FLOAT) + into
    low[...] = grad[...].astype(BFLOAT)
    sums[...] = totals
    grad_mixed = dot(low[...], weights[:, queries.shape[1] :]).astype(BFLOAT)
    for i in range(queries.shape[1] // HEAD_DIM):
        one, two, three = head_backward(
            head(queries, i),
            head(keyvals, 2 * i),
            head(keyvals, 2 * i + 1),
            allowed,
            grad_mixed[:, i * HEAD_DIM : (i + 1) * HEAD_DIM],
        )
        grad_queries[:, i * HEAD_DIM : (i + 1) * HEAD_DIM] = one
        grad_keyvals[:, 2 * i * HEAD_DIM : (2 * i + 1) * HEAD_DIM] = two
        grad_keyvals[:, (2 * i + 1) * HEAD_DIM : (2 * i + 2) * HEAD_DIM] = three
    part[...] = dot_right(grad_queries[...], weights[:, : queries.shape[1]]).astype(BFLOAT)


def keyval_backward_kernel(grad_keyvals, weights, part):
    part[...] = dot_right(grad_keyvals[...], weights[...]).astype(BFLOAT)


def self_backward_kernel(
    decoder, grad_enc, own_enc, other_enc, grad_dec, own_dec, other_dec, stream, norms, qkv, mask,
    own, other, grad, low, sums, grad_qkv, part,
):
    allowed = mask[...] > 0.5

    @pl.when(decoder[0] == 1)
    def _():
        into, totals = norm_backward(add_parts(own_dec, other_dec), stream[...], norms[1:2])
        grad[...] = grad_dec[...] + into
        sums[...] = totals

    @pl.when(decoder[0] == 0)
    def _():
        into, totals = norm_backward(add_parts(own_enc, other_enc), stream[...], norms[2:3])
        grad[...] = grad_enc[...] + into
        sums[...] = totals

    low[...] = grad[...].astype(BFLOAT)
    quarter = qkv.shape[1] // 6
    width = 3 * quarter
    total = None
    for side, weights in enumerate((own, other)):
        grad_mixed = dot(low[...], weights[:, width : width + quarter]).astype(BFLOAT)
        first = side * quarter // HEAD_DIM
        for j in range(quarter // HEAD_DIM):
            i = first + j
            grads = head_backward(
                head(qkv, 3 * i),
                head(qkv, 3 * i + 1),
                head(qkv, 3 * i + 2),
                allowed,
                grad_mixed[:, j * HEAD_DIM : (j + 1) * HEAD_DIM],
            )
            for k in range(3):
                grad_qkv[:, (3 * i + k) * HEAD_DIM : (3 * i + k + 1) * HEAD_DIM] = grads[k]
        term = dot_right(grad_qkv[:, side * width : (side + 1) * width], weights[:, :width])
        total = term if total is None else total + term
    part[...] = total.astype(BFLOAT)


def input_backward_kernel(grad, own, other, stream, norms, grad_input, sums):
    into, totals = norm_backward(add_parts(own, other), stream[...], norms[0:1])
    grad_input[...] = grad[...] + into
    sums[...] = totals


def early_weights_kernel(
    decoder, rows_enc, rows_dec, hidden_enc, hidden_dec, low_enc, low_dec, active_enc, active_dec,
    rows_two, queries, low_two, mixed, memory, keyvals, out, scratch,
):
    hidden = hidden_enc.shape[1]
    half = queries.shape[1]

    @pl.when(decoder[0] == 1)
    def _():
        out[:, :hidden] = dot_left(rows_dec[...], hidden_dec[...]).astype(BFLOAT)
        out[:, hidden : 2 * hidden] = dot_left(low_dec[...], active_dec[...]).astype(BFLOAT)
        scratch[:, :half] = dot_left(rows_two[...], queries[...])
        scratch[:, half:] = dot_left(low_two[...], mixed[...])

    @pl.when(decoder[0] == 0)
    def _():
        out[:, :hidden] = dot_left(rows_enc[...], hidden_enc[...]).astype(BFLOAT)
        out[:, hidden : 2 * hidden] = dot_left(low_enc[...], active_enc[...]).astype(BFLOAT)
        scratch[...] = dot_left(memory[...], keyvals[...])

    depth = out.shape[0]
    piece = depth // 32
    for i in range(16):
        for j in range(2):
            out[(2 * i + j) * piece : (2 * i + j + 1) * piece, 2 * hidden :] = scratch[
                j * depth // 2 + i * piece : j * depth // 2 + (i + 1) * piece, :
            ].astype(BFLOAT)


def attn_weights_kernel(rows, grad_qkv, low, mixed, norm_grads, own, other):
    quarter = mixed.shape[1] // 2
    width = 3 * quarter
    for side, out in enumerate((own, other)):
        out[:, :width] = dot_left(
            rows[...], grad_qkv[:, side * width : (side + 1) * width]
        ).astype(BFLOAT)
        out[:, width : width + quarter] = dot_left(
            low[...], mixed[:, side * quarter : (side + 1) * quarter]
        ).astype(BFLOAT)
    own[:, width + quarter :] = norm_grads[...]


def gather_plane(block):
    return lax.all_gather(block, PLANE, axis=0, tiled=True)


def scatter_plane(block):
    return lax.psum_scatter(block, PLANE, scatter_dimension=0, tiled=True)


VMEM = pl.BlockSpec(memory_space=pltpu.VMEM)
SMEM = pl.BlockSpec(memory_space=pltpu.SMEM)
LIMIT = pltpu.CompilerParams(vmem_limit_bytes=50 * 1024 * 1024)


def low_of(*dims):
    return jax.ShapeDtypeStruct(dims, BFLOAT)


def full_of(*dims):
    return jax.ShapeDtypeStruct(dims, FLOAT)


def run(kernel, outs, *operands, flops=0, scratch=(), flag=False, specs=None):
    specs = specs or {}
    in_specs = [specs.get(i, VMEM) for i in range(len(operands))]
    if flag:
        in_specs[0] = SMEM
    moved = sum(o.size * o.dtype.itemsize for o in (*operands, *outs))
    return pl.pallas_call(
        kernel,
        out_shape=list(outs),
        in_specs=in_specs,
        out_specs=[VMEM] * len(outs),
        scratch_shapes=list(scratch),
        compiler_params=LIMIT,
        cost_estimate=pl.CostEstimate(flops=flops, bytes_accessed=moved, transcendentals=0),
    )(*operands)


def shards(
    embedded,
    cotangent,
    lengths,
    attn_qkv,
    attn_out,
    ffn_up,
    ffn_down,
    norm_gain,
    norm_bias,
    cross_query,
    cross_kv,
    cross_out,
):
    is_decoder = lax.axis_index("s") == 1
    first_half = lax.axis_index("h") == 0
    core = lax.axis_index("c")

    def pick(flag, yes, no):
        return jnp.where(flag, yes, no)

    def own_row(pair):
        mine = pick(first_half, pair[0], pair[1])
        got = swap(pick(first_half, pair[1], pair[0]), "h")
        half = jnp.concatenate([pick(first_half, mine, got), pick(first_half, got, mine)])
        return lax.all_gather(half, "c", axis=0, tiled=True)

    def to_owners(row):
        half = lax.dynamic_slice_in_dim(row, core * 2 * QUARTER, 2 * QUARTER, 0)
        low, high = half[:QUARTER], half[QUARTER:]
        mine = pick(first_half, low, high)
        got = swap(pick(first_half, high, low), "h")
        return jnp.stack([pick(first_half, mine, got), pick(first_half, got, mine)])

    norms = jnp.concatenate([norm_gain[0], norm_bias[0]]).T
    norms = jnp.pad(norms, ((0, 0), (0, 128 - norms.shape[1])))
    own_attn = jnp.concatenate([attn_qkv[0], attn_out[0].T], axis=1)
    own_ffn = jnp.concatenate([ffn_up[0], ffn_down[0].T], axis=1)
    query_out = jnp.concatenate([cross_query, cross_out.T], axis=1)
    kept = pick(is_decoder, query_out, cross_kv)
    got = swap(pick(is_decoder, cross_kv, query_out), "s")
    own_cross = jnp.concatenate([pick(is_decoder, got, kept), pick(is_decoder, kept, got)])
    other_attn = swap(own_attn, "h")
    other_ffn = swap(own_ffn, "h")
    other_cross = swap(own_cross, "h")
    qkv_width = attn_qkv.shape[2]
    out_width = attn_out.shape[1]
    ff_width = ffn_up.shape[2]
    cross_width = cross_kv.shape[1]
    attn_own = gather_ring_plane(jnp.concatenate([own_attn, norms], axis=1), ("z", "x"))
    attn_other = gather_ring_plane(other_attn, ("x", "z"))
    half_cross = cross_width // 2
    key_value_pack = jnp.concatenate([own_cross, other_cross], axis=1)
    query_out_pack = jnp.concatenate(
        [
            own_cross[:, :half_cross],
            other_cross[:, :half_cross],
            own_cross[:, half_cross:],
            other_cross[:, half_cross:],
        ],
        axis=1,
    )
    cross_pack = pick(is_decoder, query_out_pack, key_value_pack)
    late_whole = gather_plane(
        jnp.concatenate(
            [
                own_ffn[:, :ff_width],
                other_ffn[:, :ff_width],
                own_ffn[:, ff_width:],
                other_ffn[:, ff_width:],
                cross_pack,
            ],
            axis=1,
        )
    )
    attn_width = qkv_width + out_width
    norms = attn_own[:, attn_width:][:, :8].T.astype(FLOAT)
    decoder = lax.axis_index("s").reshape(1).astype(jnp.int32)

    row_lengths = pick(first_half, lengths[:, 0, 0], lengths[:, 1, 0])
    source_pair = segment_ids(row_lengths[0])
    target_pair = segment_ids(row_lengths[1])
    own_pair = pick(is_decoder, target_pair, source_pair)
    positions = jnp.asarray(ORDER)
    ordered = (positions[None, :] <= positions[:, None]) | jnp.logical_not(is_decoder)
    allowed_self = ((own_pair[:, None] == own_pair[None, :]) & ordered).astype(BFLOAT)
    allowed_cross = (target_pair[:, None] == source_pair[None, :]).astype(BFLOAT)

    values = own_row(embedded[0]).astype(FLOAT)
    grad_out = own_row(cotangent[0])
    width = values.shape[1]
    hidden_width = 2 * ff_width
    steps = 4
    block = hidden_width // steps
    row_block = pl.BlockSpec((ROW_LEN, width), lambda i: (0, 0))
    norm_block = pl.BlockSpec((8, width), lambda i: (0, 0))
    up_block = pl.BlockSpec((width, block), lambda i: (0, i))
    down_block = pl.BlockSpec((width, block), lambda i: (0, i + steps))
    hidden_block = pl.BlockSpec((ROW_LEN, block), lambda i: (0, i))
    ffn_flops = 4 * ROW_LEN * width * hidden_width

    cross_whole = (
        late_whole[:, 4 * ff_width :]
        .reshape(-1, 2, cross_query.shape[0], 2 * cross_width)
        .swapaxes(0, 1)
        .reshape(width, 2 * cross_width)
    )

    def ffn_forward(stream, own, other):
        return pl.pallas_call(
            ffn_forward_kernel,
            grid=(steps,),
            out_shape=[
                full_of(ROW_LEN, width),
                low_of(ROW_LEN, width),
                full_of(ROW_LEN, hidden_width),
                low_of(ROW_LEN, hidden_width),
                low_of(ROW_LEN, width),
            ],
            in_specs=[row_block, row_block, row_block, norm_block, up_block, down_block],
            out_specs=[row_block, row_block, hidden_block, hidden_block, row_block],
            scratch_shapes=[pltpu.VMEM((ROW_LEN, width), FLOAT)],
            compiler_params=LIMIT,
            cost_estimate=pl.CostEstimate(
                flops=ffn_flops, bytes_accessed=14 * 1024 * 1024, transcendentals=0
            ),
        )(stream, own, other, norms, late_whole, late_whole)

    rows_one, qkv, mixed_one, part = run(
        self_forward_kernel,
        [
            low_of(ROW_LEN, width),
            low_of(ROW_LEN, 2 * qkv_width),
            low_of(ROW_LEN, 2 * out_width),
            low_of(ROW_LEN, width),
        ],
        values, norms, attn_own, attn_other, allowed_self,
        flops=10 * ROW_LEN * width * out_width * 2,
    )
    got = swap(part, "c")

    after_self, rows_enc, hidden_enc, active_enc, part_enc = ffn_forward(values, part, got)
    encoded, memory, keyvals = run(
        memory_kernel,
        [full_of(ROW_LEN, width), low_of(ROW_LEN, width), low_of(ROW_LEN, 2 * cross_width)],
        after_self, part_enc, swap(part_enc, "c"), norms, cross_whole,
        flops=4 * ROW_LEN * width * cross_width,
    )
    keyvals = lax.ppermute(keyvals, "s", [(0, 1)])

    after_two, rows_two, queries = run(
        query_kernel,
        [full_of(ROW_LEN, width), low_of(ROW_LEN, width), low_of(ROW_LEN, cross_width)],
        values, part, got, norms, cross_whole,
        flops=2 * ROW_LEN * width * cross_width,
    )
    mixed_two, part_two = run(
        cross_forward_kernel,
        [low_of(ROW_LEN, cross_width), low_of(ROW_LEN, width)],
        queries, keyvals, allowed_cross, cross_whole,
        flops=4 * ROW_LEN * width * cross_width,
    )
    after_cross, rows_dec, hidden_dec, active_dec, part_dec = ffn_forward(
        after_two, part_two, swap(part_two, "c")
    )
    decoded = after_cross + part_dec.astype(FLOAT) + swap(part_dec, "c").astype(FLOAT)
    outputs = to_owners(pick(is_decoder, decoded.astype(BFLOAT), memory))

    grad_hidden_dec, part = pl.pallas_call(
        ffn_backward_kernel,
        grid=(steps,),
        out_shape=[low_of(ROW_LEN, hidden_width), low_of(ROW_LEN, width)],
        in_specs=[row_block, hidden_block, up_block, down_block],
        out_specs=[hidden_block, row_block],
        scratch_shapes=[pltpu.VMEM((ROW_LEN, width), FLOAT)],
        compiler_params=LIMIT,
        cost_estimate=pl.CostEstimate(flops=ffn_flops, bytes_accessed=12 * 1024 * 1024, transcendentals=0),
    )(grad_out, hidden_dec, late_whole, late_whole)
    grad_dec, low_two, sums_two_dec, grad_queries, grad_keyvals, part_two = run(
        cross_backward_kernel,
        [
            full_of(ROW_LEN, width),
            low_of(ROW_LEN, width),
            full_of(8, width),
            low_of(ROW_LEN, cross_width),
            low_of(ROW_LEN, 2 * cross_width),
            low_of(ROW_LEN, width),
        ],
        grad_out, part, swap(part, "c"), after_cross, norms, queries, keyvals, allowed_cross,
        cross_whole,
        flops=8 * ROW_LEN * width * cross_width,
    )
    grad_keyvals = lax.ppermute(grad_keyvals, "s", [(1, 0)])
    got_two = swap(part_two, "c")

    (part,) = run(
        keyval_backward_kernel, [low_of(ROW_LEN, width)], grad_keyvals, cross_whole,
        flops=4 * ROW_LEN * width * cross_width,
    )
    grad_enc, low_enc, sums_one_enc, grad_hidden_enc, part_enc = pl.pallas_call(
        memory_ffn_backward_kernel,
        grid=(steps,),
        out_shape=[
            full_of(ROW_LEN, width),
            low_of(ROW_LEN, width),
            full_of(8, width),
            low_of(ROW_LEN, hidden_width),
            low_of(ROW_LEN, width),
        ],
        in_specs=[
            row_block, row_block, row_block, row_block, norm_block, hidden_block, up_block, down_block
        ],
        out_specs=[row_block, row_block, norm_block, hidden_block, row_block],
        scratch_shapes=[pltpu.VMEM((ROW_LEN, width), FLOAT)],
        compiler_params=LIMIT,
        cost_estimate=pl.CostEstimate(flops=ffn_flops, bytes_accessed=15 * 1024 * 1024, transcendentals=0),
    )(grad_out, part, swap(part, "c"), encoded, norms, hidden_enc, late_whole, late_whole)
    got_enc = swap(part_enc, "c")

    (grad_early,) = run(
        early_weights_kernel,
        [low_of(width, 2 * hidden_width + 2 * cross_width)],
        decoder, rows_enc, rows_dec, grad_hidden_enc, grad_hidden_dec, low_enc, grad_out,
        active_enc, active_dec, rows_two, grad_queries, low_two, mixed_two, memory, grad_keyvals,
        flops=2 * ffn_flops, flag=True,
        scratch=[pltpu.VMEM((width, 2 * cross_width), FLOAT)],
    )
    grad_early = scatter_plane(grad_early)
    grad_ffn = grad_early[:, : 2 * hidden_width]
    grad_cross = grad_early[:, 2 * hidden_width :]

    grad_self, low_self, sums_last, grad_qkv, part = run(
        self_backward_kernel,
        [
            full_of(ROW_LEN, width),
            low_of(ROW_LEN, width),
            full_of(8, width),
            low_of(ROW_LEN, 2 * qkv_width),
            low_of(ROW_LEN, width),
        ],
        decoder, grad_enc, part_enc, got_enc, grad_dec, part_two, got_two, after_self, norms, qkv,
        allowed_self, attn_own, attn_other,
        flops=20 * ROW_LEN * width * out_width * 2, flag=True,
    )
    grad_input, sums_zero = run(
        input_backward_kernel,
        [full_of(ROW_LEN, width), full_of(8, width)],
        grad_self, part, swap(part, "c"), values, norms,
    )
    grad_embedded = to_owners(grad_input)
    sums_one = pick(is_decoder, sums_last, sums_one_enc)
    sums_two = pick(is_decoder, sums_two_dec, sums_last)
    norm_grads = jnp.stack(
        [sums_zero[0], sums_one[0], sums_two[0], sums_zero[1], sums_one[1], sums_two[1]]
    ).T
    norm_grads = jnp.pad(norm_grads, ((0, 0), (0, 128 - norm_grads.shape[1]))).astype(BFLOAT)
    attn_own_grad, attn_other_grad = run(
        attn_weights_kernel,
        [low_of(width, attn_width + 128), low_of(width, attn_width)],
        rows_one, grad_qkv, low_self, mixed_one, norm_grads,
        flops=8 * ROW_LEN * width * out_width * 2,
    )
    attn_own_grad = scatter_ring_plane(attn_own_grad, ("z", "x"))
    attn_other_grad = scatter_ring_plane(attn_other_grad, ("x", "z"))

    def sum_halves(pairs):
        own = jnp.concatenate([own for own, _ in pairs], axis=1)
        other = jnp.concatenate([other for _, other in pairs], axis=1)
        return own.astype(FLOAT) + swap(other.astype(BFLOAT), "h").astype(FLOAT)

    def halves(block, start, width):
        return (block[:, start : start + width], block[:, start + width : start + 2 * width])

    total_ffn = sum_halves([halves(grad_ffn, 0, ff_width), halves(grad_ffn, 2 * ff_width, ff_width)])
    total_attn = sum_halves(
        [
            (attn_own_grad[:, :attn_width], attn_other_grad),
            (attn_own_grad[:, attn_width:], attn_own_grad[:, attn_width:]),
        ]
    )
    cross_pairs = [
        (pick(is_decoder, as_dec, as_enc))
        for as_dec, as_enc in zip(
            [
                jnp.concatenate([grad_cross[:, :half_cross], grad_cross[:, cross_width : cross_width + half_cross]], axis=1),
                jnp.concatenate([grad_cross[:, half_cross:cross_width], grad_cross[:, cross_width + half_cross :]], axis=1),
            ],
            halves(grad_cross, 0, cross_width),
        )
    ]
    total_cross = sum_halves([tuple(cross_pairs)])
    rows_cross = cross_query.shape[0]
    low_part, high_part = total_cross[:rows_cross], total_cross[rows_cross:]
    keep_part = pick(is_decoder, high_part, low_part)
    got_part = swap(pick(is_decoder, low_part, high_part).astype(BFLOAT), "s").astype(FLOAT)
    final_query_out = pick(is_decoder, keep_part, got_part)
    final_keyval = pick(is_decoder, got_part, keep_part)

    total_norm = total_attn[:, qkv_width + out_width :][:, :6].T
    return (
        outputs[None],
        grad_embedded[None],
        total_attn[:, :qkv_width][None],
        total_attn[:, qkv_width : qkv_width + out_width].T[None],
        total_ffn[:, :ff_width][None],
        total_ffn[:, ff_width:].T[None],
        total_norm[:3][None],
        total_norm[3:][None],
        final_query_out[:, :half_cross],
        final_keyval,
        final_query_out[:, half_cross:].T,
    )


def solution(mesh):
    fine = Mesh(mesh.devices.reshape(2, 4, 4, 2, 2), AXES)
    tokens = ("x", "z", "h", "c")
    tensor = ("h", "c")
    whole = ("s", "x", "z")
    return jax.shard_map(
        shards,
        mesh=fine,
        in_specs=(
            P("s", None, tokens, None),
            P("s", None, tokens, None),
            P(None, None, PLANE, None),
            P("s", PLANE, tensor),
            P("s", tensor, PLANE),
            P("s", PLANE, tensor),
            P("s", tensor, PLANE),
            P("s", None, PLANE),
            P("s", None, PLANE),
            P(whole, tensor),
            P(whole, tensor),
            P(tensor, whole),
        ),
        out_specs=(
            P("s", None, tokens, None),
            P("s", None, tokens, None),
            P("s", PLANE, tensor),
            P("s", tensor, PLANE),
            P("s", PLANE, tensor),
            P("s", tensor, PLANE),
            P("s", None, PLANE),
            P("s", None, PLANE),
            P(whole, tensor),
            P(whole, tensor),
            P(tensor, whole),
        ),
        check_vma=False,
    )
```

time: 551 us -> 364 us (0.66)
  waiting for transfers between devices: 339 us -> 139 us
  Pallas kernels: 0 us -> 83.1 us
  matrix products: 69.5 us -> 0 us
  starting transfers between devices: 39.8 us -> 74.7 us
  other arithmetic: 38.8 us -> 12.9 us
  local copies, waits for them, and re-layouts: 34.5 us -> 27.6 us
    reduce_scatter x3 -> x1, waiting for transfers between devices: 156 us -> 2.87 us  [scatter_plane(): return lax.psum_scatter(block, PLANE, scatter_dimension=0, tiled=True)]
    all_gather x3 -> x1, waiting for transfers between devices: 128 us -> 19.1 us  [gather_plane(): return lax.all_gather(block, PLANE, axis=0, tiled=True)]
    pallas_call x0 -> x14, Pallas kernels: none -> 83.1 us  [the longest x10 50.5 us: run(): pl.pallas_call(kernel, out_shape=list(outs), in_specs=in_specs, out_specs...]
    ppermute x1 -> x29, waiting for transfers between devices: 6.07 us -> 70.5 us  [the longest x28 64.6 us: shift(): lax.ppermute(block, axis, [(i, (i + distance) % size) for i in range(size)])]
    dot_general x35 -> x0, matrix products: 64.3 us -> none  [the longest x9 20.3 us: dot(): return jnp.dot(left, right, preferred_element_type=FLOAT)]
    ppermute x1 -> x29, starting transfers between devices: 4.2 us -> 47 us  [the longest x28 43.6 us: shift(): lax.ppermute(block, axis, [(i, (i + distance) % size) for i in range(size)])]
    concatenate x2 -> x6, other arithmetic: 11.7 us -> 0.25 us  [the longest x2 0.11 us: scatter_ring(): jnp.concatenate([before[:half].astype(FLOAT), before[half:].astype(FLOAT)...]
    reduce_sum x12 -> x0, other arithmetic: 8.96 us -> none  [the longest x3 4.16 us: norm_backward(): jnp.sum(grad_out * normed, axis=0)]
  transfers between devices with their start and end apart: 29 -> 53, of which waited for: 20 -> 32; matrix products, arithmetic and copies ran while one was open for 20% -> 6% of each run, Pallas kernels for 0% -> 8%
where the time goes in v2:
time: 364 us; the launch traced here: 357 us
  waiting for transfers between devices  139 us (38%)
  Pallas kernels  83.1 us (23%)
  starting transfers between devices  74.7 us (21%)
  local copies, waits for them, and re-layouts  27.6 us (8%)
  between operations  15.2 us (4%)
  other arithmetic  12.9 us (4%)
  blocking collectives  4.54 us (1%)
    ppermute x28, waiting for transfers between devices, shift(): lax.ppermute(block, axis, [(i, (i + distance) % size) for i in range(size)])  64.6 us
    pallas_call x10, Pallas kernels, run(): pl.pallas_call(kernel, out_shape=list(outs), in_specs=in_specs, out_specs...  50.5 us
    ppermute x28, starting transfers between devices, shift(): lax.ppermute(block, axis, [(i, (i + distance) % size) for i in range(size)])  43.6 us
    ppermute x21, waiting for transfers between devices, swap(): return lax.ppermute(block, axis, [(0, 1), (1, 0)])  31.8 us
    ppermute x21, starting transfers between devices, swap(): return lax.ppermute(block, axis, [(0, 1), (1, 0)])  26.3 us
    all_gather x1, waiting for transfers between devices, gather_plane(): return lax.all_gather(block, PLANE, axis=0, tiled=True)  19.1 us
    pallas_call x2, Pallas kernels, ffn_forward(): pl.pallas_call(ffn_forward_kernel, grid=(steps,), out_shape=[full_of(ROW_...  16.5 us
    unnamed x85, local copies, waits for them, and re-layouts  14.8 us
  transfers between devices with their start and end apart: 53, of which 32 were waited for; matrix products, arithmetic and copies ran while one was open for 6% of the time, Pallas kernels for 8%

profile of v2, /device:TPU:0, one launch (start us, length us, event | category | flops | bytes accessed | tf_op | source)
XLA Modules:
  0.0 356.9 jit_solution(11509703396849399034)
XLA Ops:
  8.4 3.4 collective-permute-start.17
  14.2 5.0 %collective-permute-done.18 = bf16[32,512]{1,0:T(8,128)(2,1)S(1)} collective-permute-done((bf16[32,512]{1,0:T(8,128)(2,1)S(1)}, bf16[32,512]{1,0:T(8,128)(2,1)S(1)}, u32[]{:S(2)}, u32[]{:S(2)}) %collective-permute-start.18) | collective-permute-done | bytes 32800 | tf_op jit(solution)/shard_map/ppermute | solution.py:28
  21.8 3.9 %collective-permute-done.19 = bf16[64,512]{1,0:T(8,128)(2,1)S(1)} collective-permute-done((bf16[64,512]{1,0:T(8,128)(2,1)S(1)}, bf16[64,512]{1,0:T(8,128)(2,1)S(1)}, u32[]{:S(2)}, u32[]{:S(2)}) %collective-permute-start.19) | collective-permute-done | bytes 65568 | tf_op jit(solution)/shard_map/ppermute | solution.py:28
  27.9 4.1 %collective-permute-start.1 = (bf16[64,1152]{1,0:T(8,128)(2,1)S(1)}, bf16[64,1152]{1,0:T(8,128)(2,1)S(1)}, u32[]{:S(2)}, u32[]{:S(2)}) collective-permute-start(bf16[64,1152]{1,0:T(8,128)(2,1)S(1)} %fusion.17), channel_id=1, source_target_pairs={{0,12},{4,0},{8,4},{12,8},{1,13},{5,1},{9,5},{13,9},{2,14},{6,2},{... | collective-permute-start | bytes 442376 | tf_op jit(solution)/shard_map/ppermute | solution.py:33
  42.2 2.8 collective-permute-start.9
  47.0 2.4 collective-permute-start.4
  51.8 3.5 collective-permute-done.10
  55.3 2.9 collective-permute-done.11
  58.2 2.3 collective-permute-start.12
  61.0 9.5 %collective-permute-done.4 = bf16[4,64,1152]{2,1,0:T(8,128)(2,1)S(1)} collective-permute-done((bf16[4,64,1152]{2,1,0:T(8,128)(2,1)S(1)}, bf16[4,64,1152]{2,1,0:T(8,128)(2,1)S(1)}, u32[]{:S(2)}, u32[]{:S(2)}) %collective-permute-start.4) | collective-permute-done | bytes 589856 | tf_op jit(solution)/shard_map/ppermute | solution.py:33
  70.6 3.3 collective-permute-start.7
  74.1 2.5 collective-permute-start.15
  77.3 9.8 %collective-permute-done.7 = bf16[2,64,1152]{2,1,0:T(8,128)(2,1)S(1)} collective-permute-done((bf16[2,64,1152]{2,1,0:T(8,128)(2,1)S(1)}, bf16[2,64,1152]{2,1,0:T(8,128)(2,1)S(1)}, u32[]{:S(2)}, u32[]{:S(2)}) %collective-permute-start.7) | collective-permute-done | bytes 294944 | tf_op jit(solution)/shard_map/ppermute | solution.py:33
  87.1 3.7 %collective-permute-done.6 = bf16[2,64,1152]{2,1,0:T(8,128)(2,1)S(1)} collective-permute-done((bf16[2,64,1152]{2,1,0:T(8,128)(2,1)S(1)}, bf16[2,64,1152]{2,1,0:T(8,128)(2,1)S(1)}, u32[]{:S(2)}, u32[]{:S(2)}) %collective-permute-start.6) | collective-permute-done | bytes 294944 | tf_op jit(solution)/shard_map/ppermute | solution.py:33
  95.4 6.0 %shard_map.212 = (bf16[256,1024]{1,0:T(8,128)(2,1)S(1)}, bf16[256,1536]{1,0:T(8,128)(2,1)S(1)}, bf16[256,512]{1,0:T(8,128)(2,1)S(1)}, bf16[256,1024]{1,0:T(8,128)(2,1)S(1)}) custom-call(f32[256,1024]{1,0:T(8,128)S(1)} %convert_element_type.190.stream, f32[8,1024]{1,0:T(8,128)S(1)} %convert_bitcast_fusion.norms, bf16[1024,1152]{1,0:T(8,128)(2,1)} %bitcast.208, ...), custom_call_target="tpu_custom_call" | custom-call | flops 1342177280 | bytes 7766016 | tf_op jit(solution)/shard_map/pallas_call | solution.py:443
  105.7 19.1 %all-gather.2.cloned.1.call-done.up.down = bf16[1024,5120]{1,0:T(8,128)(2,1)} async-done(((bf16[64,5120]{1,0:T(8,128)(2,1)}), bf16[1024,5120]{1,0:T(8,128)(2,1)}) %all-gather.2.cloned.1.call-update) | async-done | bytes 10485776 | tf_op jit(solution)/shard_map/all_gather | solution.py:417
  124.9 8.2 %shard_map.214 = (f32[256,1024]{1,0:T(8,128)S(1)}, bf16[256,1024]{1,0:T(8,128)(2,1)S(1)}, f32[256,2048]{1,0:T(8,128)}, bf16[256,2048]{1,0:T(8,128)(2,1)}, bf16[256,1024]{1,0:T(8,128)(2,1)S(1)}) custom-call(f32[256,1024]{1,0:T(8,128)} %copy-done.2, bf16[256,1024]{1,0:T(8,128)(2,1)S(1)} %get-tuple-element.55.own, ...), custom_call_target="tpu_custom_call" | custom-call | flops 2147483648 | bytes 14680064 | tf_op jit(solution)/shard_map/pallas_call | solution.py:563
  136.6 3.1 shard_map.215
  140.5 3.4 collective-permute-start.21
  143.9 2.8 collective-permute-start.25
  146.8 2.5 shard_map.213
  150.3 5.9 %collective-permute-done.21.keyvals = bf16[256,1024]{1,0:T(8,128)(2,1)S(1)} collective-permute-done((bf16[256,1024]{1,0:T(8,128)(2,1)S(1)}, bf16[256,1024]{1,0:T(8,128)(2,1)S(1)}, u32[]{:S(2)}, u32[]{:S(2)}) %collective-permute-start.21) | collective-permute-done | bytes 524320 | tf_op jit(solution)/shard_map/ppermute | solution.py:602
  156.2 2.9 shard_map.216
  161.2 2.4 all_gather.11.low.cotangent.low_dec
  163.6 8.3 %shard_map.217 = (f32[256,1024]{1,0:T(8,128)S(1)}, bf16[256,1024]{1,0:T(8,128)(2,1)S(1)}, f32[256,2048]{1,0:T(8,128)}, bf16[256,2048]{1,0:T(8,128)(2,1)}, bf16[256,1024]{1,0:T(8,128)(2,1)}) custom-call(f32[256,1024]{1,0:T(8,128)} %copy-done.14, bf16[256,1024]{1,0:T(8,128)(2,1)S(1)} %get-tuple-element.61.own, ...), custom_call_target="tpu_custom_call" | custom-call | flops 2147483648 | bytes 14680064 | tf_op jit(solution)/shard_map/pallas_call | solution.py:563
  172.9 6.9 %shard_map.218 = (bf16[256,2048]{1,0:T(8,128)(2,1)S(1)}, bf16[256,1024]{1,0:T(8,128)(2,1)S(1)}) custom-call(bf16[256,1024]{1,0:T(8,128)(2,1)S(1)} %all_gather.11.low.cotangent.low_dec, f32[256,2048]{1,0:T(8,128)} %get-tuple-element.65.hidden, bf16[1024,5120]{1,0:T(8,128)(2,1)} %all-gather.2.cloned.1.call-done.up.down, ...), custom_call_target="tpu_custom_call" | custom-call | flops 2147483648 | bytes 12582912 | tf_op jit(solution)/shard_map/pallas_call | solution.py:622
  181.8 8.2 %shard_map.219 = (f32[256,1024]{1,0:T(8,128)}, bf16[256,1024]{1,0:T(8,128)(2,1)S(1)}, f32[8,1024]{1,0:T(8,128)S(1)}, bf16[256,512]{1,0:T(8,128)(2,1)S(1)}, bf16[...) custom-call(bf16[256,1024]{1,0:T(8,128)(2,1)S(1)} %all_gather.11.low.cotangent.low_dec, ...), custom_call_target="tpu_custom_call" | custom-call | flops 1073741824 | bytes 8585216 | tf_op jit(solution)/shard_map/pallas_call | solution.py:443
  191.3 14.5 %collective-permute-done.27.grad_keyvals.keyvals = bf16[256,1024]{1,0:T(8,128)(2,1)S(1)} collective-permute-done((bf16[256,1024]{1,0:T(8,128)(2,1)S(1)}, bf16[256,1024]{1,0:T(8,128)(2,1)S(1)}, u32[]{:S(2)}, u32[]{:S(2)}) %collective-permute-start.27) | collective-permute-done | bytes 524320 | tf_op jit(solution)/shard_map/ppermute | solution.py:646
  208.6 9.2 %shard_map.221 = (f32[256,1024]{1,0:T(8,128)S(1)}, bf16[256,1024]{1,0:T(8,128)(2,1)S(1)}, f32[8,1024]{1,0:T(8,128)S(1)}, bf16[256,2048]{1,0:T(8,128)(2,1)}, bf16[256,1024]{1,0:T(8,128)(2,1)S(1)}) custom-call(bf16[256,1024]{1,0:T(8,128)(2,1)S(1)} %all_gather.11.low.cotangent.low_dec, bf16[256,1024]{1,0:T(8,128)(2,1)S(1)} %shard_map.220.own, ...), custom_call_target="tpu_custom_call" | custom-call | flops 2147483648 | bytes 15728640 | tf_op jit(solution)/shard_map/pallas_call | solution.py:653
  218.9 9.7 %shard_map.225 = bf16[1024,5120]{1,0:T(8,128)(2,1)} custom-call(s32[1]{0:T(128)} %bitcast.45.decoder, bf16[256,1024]{1,0:T(8,128)(2,1)S(1)} %get-tuple-element.88.rows_enc, bf16[256,1024]{1,0:T(8,128)(2,1)S(1)} %get-tuple-element.89.rows_dec, bf16[256,2048]{1,0:T(8,128)(2,1)} %get-tuple-element.90.hidden_enc, bf16[256,2048]{1,0:T(8,128)(2,1)} %copy-done.12, ...), custom_call_target="tpu_custom_call" | custom-call | flops 4294967296 | bytes 19398660 | tf_op jit(solution)/shard_map/pallas_call | solution.py:443
  233.4 11.8 %shard_map.222 = (f32[256,1024]{1,0:T(8,128)}, bf16[256,1024]{1,0:T(8,128)(2,1)S(1)}, f32[8,1024]{1,0:T(8,128)S(1)}, bf16[256,1536]{1,0:T(8,128)(2,1)}, bf16[256,1024]{1,0:T(8,128)(2,1)S(1)}) custom-call(s32[1]{0:T(128)} %bitcast.45.decoder, f32[256,1024]{1,0:T(8,128)} %copy-done.15, bf16[256,1024]{1,0:T(8,128)(2,1)S(1)} %get-tuple-element.71.own_enc, ...), custom_call_target="tpu_custom_call" | custom-call | flops 2684354560 | bytes 13565956 | tf_op jit(solution)/shard_map/pallas_call | solution.py:443
  248.4 2.2 shard_map.223
  252.0 3.3 shard_map.224
  264.7 7.4 %collective-permute-done.40 = bf16[2,64,1024]{2,1,0:T(8,128)(2,1)S(1)} collective-permute-done((bf16[2,64,1024]{2,1,0:T(8,128)(2,1)S(1)}, bf16[2,64,1024]{2,1,0:T(8,128)(2,1)S(1)}, u32[]{:S(2)}, u32[]{:S(2)}) %collective-permute-start.40) | collective-permute-done | bytes 262176 | tf_op jit(solution)/shard_map/ppermute | solution.py:33
  272.9 3.0 collective-permute-start.43
  278.1 2.8 collective-permute-start.36
  281.9 2.8 collective-permute-start.32
  284.7 13.7 %collective-permute-done.43 = bf16[4,64,1024]{2,1,0:T(8,128)(2,1)S(1)} collective-permute-done((bf16[4,64,1024]{2,1,0:T(8,128)(2,1)S(1)}, bf16[4,64,1024]{2,1,0:T(8,128)(2,1)S(1)}, u32[]{:S(2)}, u32[]{:S(2)}) %collective-permute-start.43) | collective-permute-done | bytes 524320 | tf_op jit(solution)/shard_map/ppermute | solution.py:33
  298.3 2.9 collective-permute-done.41
  305.7 2.2 collective-permute-start.39
  308.2 2.2 collective-permute-start.38
  311.9 3.0 collective-permute-done.38
  314.9 3.4 collective-permute-done.37
  320.9 4.2 %collective-permute-done.47 = bf16[64,1152]{1,0:T(8,128)(2,1)S(1)} collective-permute-done((bf16[64,1152]{1,0:T(8,128)(2,1)S(1)}, bf16[64,1152]{1,0:T(8,128)(2,1)S(1)}, u32[]{:S(2)}, u32[]{:S(2)}) %collective-permute-start.47) | collective-permute-done | bytes 147488 | tf_op jit(solution)/shard_map/ppermute | solution.py:28
  327.9 2.9 reduce-scatter.2.cloned.1.call-done
  332.4 2.8 collective-permute-start.49
  341.0 2.3 collective-permute-start.48
  344.8 4.2 %collective-permute-done.48 = bf16[64,2048]{1,0:T(8,128)(2,1)S(1)} collective-permute-done((bf16[64,2048]{1,0:T(8,128)(2,1)S(1)}, bf16[64,2048]{1,0:T(8,128)(2,1)S(1)}, u32[]{:S(2)}, u32[]{:S(2)}) %collective-permute-start.48) | collective-permute-done | bytes 262176 | tf_op jit(solution)/shard_map/ppermute | solution.py:28
  (261 shorter events, 92.2 us)
Async XLA Ops:
  7.2 117.6 %all-gather.2.cloned.1.call-start = ((), (), s32[]{:S(2)}) async-start(), calls=%async_computation.1 | async-start | bytes 11141120 | tf_op jit(solution)/shard_map/all_gather | solution.py:417
  8.4 17.4 %collective-permute-start.17 = (bf16[64,2048]{1,0:T(8,128)(2,1)S(1)}, bf16[64,2048]{1,0:T(8,128)(2,1)S(1)}, u32[]{:S(2)}, u32[]{:S(2)}) collective-permute-start(bf16[64,2048]{1,0:T(8,128)(2,1)S(1)} %pad_maximum_fusion.5), channel_id=1, source_target_pairs={{0,2},{2,0},{1,3},{3,1},{4,6},{6,4},{5,7},{7,5},{8,10},{10,8},{9,1... | collective-permute-start | bytes 786440 | tf_op jit(solution)/shard_map/ppermute | solution.py:28
  12.5 6.6 %collective-permute-start.18 = (bf16[32,512]{1,0:T(8,128)(2,1)S(1)}, bf16[32,512]{1,0:T(8,128)(2,1)S(1)}, u32[]{:S(2)}, u32[]{:S(2)}) collective-permute-start(bf16[32,512]{1,0:T(8,128)(2,1)S(1)} %broadcast_select_fusion.7), channel_id=1, source_target_pairs={{0,64},{64,0},{1,65},{65,1},{2,66},{66,2},{3,67},{67,3},{4,68},{68... | collective-permute-start | bytes 98312 | tf_op jit(solution)/shard_map/ppermute | solution.py:28
  19.9 5.8 %collective-permute-start.19 = (bf16[64,512]{1,0:T(8,128)(2,1)S(1)}, bf16[64,512]{1,0:T(8,128)(2,1)S(1)}, u32[]{:S(2)}, u32[]{:S(2)}) collective-permute-start(bf16[64,512]{1,0:T(8,128)(2,1)S(1)} %pad_maximum_fusion.10), channel_id=1, source_target_pairs={{0,2},{2,0},{1,3},{3,1},{4,6},{6,4},{5,7},{7,5},{8,10},{10,8},{9,1... | collective-permute-start | bytes 196616 | tf_op jit(solution)/shard_map/ppermute | solution.py:28
  27.6 303.1 %reduce-scatter.2.cloned.1.call-start = ((), (), s32[]{:S(2)}) async-start(), calls=%async_computation.2 | async-start | bytes 11141120 | tf_op jit(solution)/shard_map/reduce_scatter | solution.py:421
  27.9 18.0 %collective-permute-start.1 = (bf16[64,1152]{1,0:T(8,128)(2,1)S(1)}, bf16[64,1152]{1,0:T(8,128)(2,1)S(1)}, u32[]{:S(2)}, u32[]{:S(2)}) collective-permute-start(bf16[64,1152]{1,0:T(8,128)(2,1)S(1)} %fusion.17), channel_id=1, source_target_pairs={{0,12},{4,0},{8,4},{12,8},{1,13},{5,1},{9,5},{13,9},{2,14},{6,2},{... | collective-permute-start | bytes 442376 | tf_op jit(solution)/shard_map/ppermute | solution.py:33
  32.0 14.9 %collective-permute-start.2 = (bf16[64,1152]{1,0:T(8,128)(2,1)S(1)}, bf16[64,1152]{1,0:T(8,128)(2,1)S(1)}, u32[]{:S(2)}, u32[]{:S(2)}) collective-permute-start(bf16[64,1152]{1,0:T(8,128)(2,1)S(1)} %fusion.17), channel_id=1, source_target_pairs={{0,8},{4,12},{8,0},{12,4},{1,9},{5,13},{9,1},{13,5},{2,10},{6,14},... | collective-permute-start | bytes 442376 | tf_op jit(solution)/shard_map/ppermute | solution.py:33
  32.0 14.9 %collective-permute-start.3 = (bf16[64,1152]{1,0:T(8,128)(2,1)S(1)}, bf16[64,1152]{1,0:T(8,128)(2,1)S(1)}, u32[]{:S(2)}, u32[]{:S(2)}) collective-permute-start(bf16[64,1152]{1,0:T(8,128)(2,1)S(1)} %fusion.17), channel_id=1, source_target_pairs={{0,4},{4,8},{8,12},{12,0},{1,5},{5,9},{9,13},{13,1},{2,6},{6,10},{... | collective-permute-start | bytes 442376 | tf_op jit(solution)/shard_map/ppermute | solution.py:33
  33.3 6.6 %collective-permute-start = (bf16[64,1024]{1,0:T(8,128)(2,1)S(1)}, bf16[64,1024]{1,0:T(8,128)(2,1)S(1)}, u32[]{:S(2)}, u32[]{:S(2)}) collective-permute-start(bf16[64,1024]{1,0:T(8,128)(2,1)S(1)} %select_bitcast_fusion.5), channel_id=1, source_target_pairs={{0,2},{2,0},{1,3},{3,1},{4,6},{6,4},{5,7},{7,5},{8,10},{10,8},{9,1... | collective-permute-start | bytes 393224 | tf_op jit(solution)/shard_map/ppermute | solution.py:28
  35.2 7.0 %collective-permute-start.8 = (bf16[64,1024]{1,0:T(8,128)(2,1)S(1)}, bf16[64,1024]{1,0:T(8,128)(2,1)S(1)}, u32[]{:S(2)}, u32[]{:S(2)}) collective-permute-start(bf16[64,1024]{1,0:T(8,128)(2,1)S(1)} %pad_maximum_fusion.9), channel_id=1, source_target_pairs={{0,2},{2,0},{1,3},{3,1},{4,6},{6,4},{5,7},{7,5},{8,10},{10,8},{9,1... | collective-permute-start | bytes 393224 | tf_op jit(solution)/shard_map/ppermute | solution.py:28
  42.2 9.6 %collective-permute-start.9 = (bf16[64,1024]{1,0:T(8,128)(2,1)S(1)}, bf16[64,1024]{1,0:T(8,128)(2,1)S(1)}, u32[]{:S(2)}, u32[]{:S(2)}) collective-permute-start(bf16[64,1024]{1,0:T(8,128)(2,1)S(1)} %collective-permute-done.8), channel_id=1, source_target_pairs={{0,48},{16,0},{32,16},{48,32},{1,49},{17,1},{33,17},{49,33},{2,50}... | collective-permute-start | bytes 393224 | tf_op jit(solution)/shard_map/ppermute | solution.py:33
  45.0 10.2 %collective-permute-start.10 = (bf16[64,1024]{1,0:T(8,128)(2,1)S(1)}, bf16[64,1024]{1,0:T(8,128)(2,1)S(1)}, u32[]{:S(2)}, u32[]{:S(2)}) collective-permute-start(bf16[64,1024]{1,0:T(8,128)(2,1)S(1)} %collective-permute-done.8), channel_id=1, source_target_pairs={{0,32},{16,48},{32,0},{48,16},{1,33},{17,49},{33,1},{49,17},{2,34}... | collective-permute-start | bytes 393224 | tf_op jit(solution)/shard_map/ppermute | solution.py:33
  45.9 12.2 %collective-permute-start.11 = (bf16[64,1024]{1,0:T(8,128)(2,1)S(1)}, bf16[64,1024]{1,0:T(8,128)(2,1)S(1)}, u32[]{:S(2)}, u32[]{:S(2)}) collective-permute-start(bf16[64,1024]{1,0:T(8,128)(2,1)S(1)} %collective-permute-done.8), channel_id=1, source_target_pairs={{0,16},{16,32},{32,48},{48,0},{1,17},{17,33},{33,49},{49,1},{2,18}... | collective-permute-start | bytes 393224 | tf_op jit(solution)/shard_map/ppermute | solution.py:33
  47.0 23.6 %collective-permute-start.4 = (bf16[4,64,1152]{2,1,0:T(8,128)(2,1)S(1)}, bf16[4,64,1152]{2,1,0:T(8,128)(2,1)S(1)}, u32[]{:S(2)}, u32[]{:S(2)}) collective-permute-start(bf16[4,64,1152]{2,1,0:T(8,128)(2,1)S(1)} %bitcast_dynamic-update-slice_fusion.6), channel_id=1, source_target_pairs={{0,48},{16,0},{32,16},{48,32},{1,49},{17,1},{33,17},{49,33},{2,50}... | collective-permute-start | bytes 1769480 | tf_op jit(solution)/shard_map/ppermute | solution.py:33
  49.4 24.5 %collective-permute-start.5 = (bf16[4,64,1152]{2,1,0:T(8,128)(2,1)S(1)}, bf16[4,64,1152]{2,1,0:T(8,128)(2,1)S(1)}, u32[]{:S(2)}, u32[]{:S(2)}) collective-permute-start(bf16[4,64,1152]{2,1,0:T(8,128)(2,1)S(1)} %bitcast_dynamic-update-slice_fusion.6), channel_id=1, source_target_pairs={{0,16},{16,32},{32,48},{48,0},{1,17},{17,33},{33,49},{49,1},{2,18}... | collective-permute-start | bytes 1769480 | tf_op jit(solution)/shard_map/ppermute | solution.py:33
  58.2 15.9 %collective-permute-start.12 = (bf16[4,64,1024]{2,1,0:T(8,128)(2,1)S(1)}, bf16[4,64,1024]{2,1,0:T(8,128)(2,1)S(1)}, u32[]{:S(2)}, u32[]{:S(2)}) collective-permute-start(bf16[4,64,1024]{2,1,0:T(8,128)(2,1)S(1)} %bitcast_dynamic-update-slice_fusion.10), channel_id=1, source_target_pairs={{0,12},{4,0},{8,4},{12,8},{1,13},{5,1},{9,5},{13,9},{2,14},{6,2},{... | collective-permute-start | bytes 1572872 | tf_op jit(solution)/shard_map/ppermute | solution.py:33
  60.5 16.1 %collective-permute-start.13 = (bf16[4,64,1024]{2,1,0:T(8,128)(2,1)S(1)}, bf16[4,64,1024]{2,1,0:T(8,128)(2,1)S(1)}, u32[]{:S(2)}, u32[]{:S(2)}) collective-permute-start(bf16[4,64,1024]{2,1,0:T(8,128)(2,1)S(1)} %bitcast_dynamic-update-slice_fusion.10), channel_id=1, source_target_pairs={{0,4},{4,8},{8,12},{12,0},{1,5},{5,9},{9,13},{13,1},{2,6},{6,10},{... | collective-permute-start | bytes 1572872 | tf_op jit(solution)/shard_map/ppermute | solution.py:33
  70.6 16.6 %collective-permute-start.7 = (bf16[2,64,1152]{2,1,0:T(8,128)(2,1)S(1)}, bf16[2,64,1152]{2,1,0:T(8,128)(2,1)S(1)}, u32[]{:S(2)}, u32[]{:S(2)}) collective-permute-start(bf16[2,64,1152]{2,1,0:T(8,128)(2,1)S(1)} %slice.317), channel_id=1, source_target_pairs={{0,48},{16,0},{32,16},{48,32},{1,49},{17,1},{33,17},{49,33},{2,50}... | collective-permute-start | bytes 884744 | tf_op jit(solution)/shard_map/ppermute | solution.py:33
  73.9 17.0 %collective-permute-start.6 = (bf16[2,64,1152]{2,1,0:T(8,128)(2,1)S(1)}, bf16[2,64,1152]{2,1,0:T(8,128)(2,1)S(1)}, u32[]{:S(2)}, u32[]{:S(2)}) collective-permute-start(bf16[2,64,1152]{2,1,0:T(8,128)(2,1)S(1)} %slice.316), channel_id=1, source_target_pairs={{0,16},{16,32},{32,48},{48,0},{1,17},{17,33},{33,49},{49,1},{2,18}... | collective-permute-start | bytes 884744 | tf_op jit(solution)/shard_map/ppermute | solution.py:33
  74.1 18.5 %collective-permute-start.15 = (bf16[2,64,1024]{2,1,0:T(8,128)(2,1)S(1)}, bf16[2,64,1024]{2,1,0:T(8,128)(2,1)}, u32[]{:S(2)}, u32[]{:S(2)}) collective-permute-start(bf16[2,64,1024]{2,1,0:T(8,128)(2,1)S(1)} %slice.320), channel_id=1, source_target_pairs={{0,12},{4,0},{8,4},{12,8},{1,13},{5,1},{9,5},{13,9},{2,14},{6,2},{... | collective-permute-start | bytes 786440 | tf_op jit(solution)/shard_map/ppermute | solution.py:33
  76.6 16.1 %collective-permute-start.14 = (bf16[2,64,1024]{2,1,0:T(8,128)(2,1)S(1)}, bf16[2,64,1024]{2,1,0:T(8,128)(2,1)}, u32[]{:S(2)}, u32[]{:S(2)}) collective-permute-start(bf16[2,64,1024]{2,1,0:T(8,128)(2,1)S(1)} %slice.319), channel_id=1, source_target_pairs={{0,4},{4,8},{8,12},{12,0},{1,5},{5,9},{9,13},{13,1},{2,6},{6,10},{... | collective-permute-start | bytes 786440 | tf_op jit(solution)/shard_map/ppermute | solution.py:33
  133.0 3.6 %collective-permute-start.20 = (bf16[256,1024]{1,0:T(8,128)(2,1)S(1)}, bf16[256,1024]{1,0:T(8,128)(2,1)S(1)}, u32[]{:S(2)}, u32[]{:S(2)}) collective-permute-start(bf16[256,1024]{1,0:T(8,128)(2,1)S(1)} %get-tuple-element.59.own), channel_id=1, source_target_pairs={{0,1},{1,0},{2,3},{3,2},{4,5},{5,4},{6,7},{7,6},{8,9},{9,8},{10,11... | collective-permute-start | bytes 1572872 | tf_op jit(solution)/shard_map/ppermute | solution.py:28
  140.5 15.7 %collective-permute-start.21 = (bf16[256,1024]{1,0:T(8,128)(2,1)S(1)}, bf16[256,1024]{1,0:T(8,128)(2,1)S(1)}, u32[]{:S(2)}, u32[]{:S(2)}) collective-permute-start(bf16[256,1024]{1,0:T(8,128)(2,1)S(1)} %get-tuple-element.60), channel_id=1, source_target_pairs={{0,64},{1,65},{2,66},{3,67},{4,68},{5,69},{6,70},{7,71},{8,72},{9,... | collective-permute-start | bytes 1572872 | tf_op jit(solution)/shard_map/ppermute | solution.py:602
  143.9 17.2 %collective-permute-start.25 = (bf16[64,1024]{1,0:T(8,128)(2,1)S(1)}, bf16[64,1024]{1,0:T(8,128)(2,1)S(1)}, u32[]{:S(2)}, u32[]{:S(2)}) collective-permute-start(bf16[64,1024]{1,0:T(8,128)(2,1)S(1)} %select_bitcast_fusion.2), channel_id=1, source_target_pairs={{0,2},{2,0},{1,3},{3,1},{4,6},{6,4},{5,7},{7,5},{8,10},{10,8},{9,1... | collective-permute-start | bytes 393224 | tf_op jit(solution)/shard_map/ppermute | solution.py:28
  159.1 4.5 %collective-permute-start.22 = (bf16[256,1024]{1,0:T(8,128)(2,1)S(1)}, bf16[256,1024]{1,0:T(8,128)(2,1)S(1)}, u32[]{:S(2)}, u32[]{:S(2)}) collective-permute-start(bf16[256,1024]{1,0:T(8,128)(2,1)S(1)} %get-tuple-element.61.own), channel_id=1, source_target_pairs={{0,1},{1,0},{2,3},{3,2},{4,5},{5,4},{6,7},{7,6},{8,9},{9,8},{10,11... | collective-permute-start | bytes 1572872 | tf_op jit(solution)/shard_map/ppermute | solution.py:28
  190.0 15.8 %collective-permute-start.27 = (bf16[256,1024]{1,0:T(8,128)(2,1)S(1)}, bf16[256,1024]{1,0:T(8,128)(2,1)S(1)}, u32[]{:S(2)}, u32[]{:S(2)}) collective-permute-start(bf16[256,1024]{1,0:T(8,128)(2,1)S(1)} %get-tuple-element.67), channel_id=1, source_target_pairs={{64,0},{65,1},{66,2},{67,3},{68,4},{69,5},{70,6},{71,7},{72,8},{73... | collective-permute-start | bytes 1572872 | tf_op jit(solution)/shard_map/ppermute | solution.py:646
  228.8 4.6 %collective-permute-start.30 = (bf16[256,1024]{1,0:T(8,128)(2,1)S(1)}, bf16[256,1024]{1,0:T(8,128)(2,1)S(1)}, u32[]{:S(2)}, u32[]{:S(2)}) collective-permute-start(bf16[256,1024]{1,0:T(8,128)(2,1)S(1)} %get-tuple-element.73.own_dec), channel_id=1, source_target_pairs={{0,1},{1,0},{2,3},{3,2},{4,5},{5,4},{6,7},{7,6},{8,9},{9,8},{10,11... | collective-permute-start | bytes 1572872 | tf_op jit(solution)/shard_map/ppermute | solution.py:28
  229.2 4.2 %collective-permute-start.29 = (bf16[256,1024]{1,0:T(8,128)(2,1)S(1)}, bf16[256,1024]{1,0:T(8,128)(2,1)}, u32[]{:S(2)}, u32[]{:S(2)}) collective-permute-start(bf16[256,1024]{1,0:T(8,128)(2,1)S(1)} %get-tuple-element.71.own_enc), channel_id=1, source_target_pairs={{0,1},{1,0},{2,3},{3,2},{4,5},{5,4},{6,7},{7,6},{8,9},{9,8},{10,11... | collective-permute-start | bytes 1572872 | tf_op jit(solution)/shard_map/ppermute | solution.py:28
  232.2 13.1 %collective-permute-start.24 = (bf16[64,1024]{1,0:T(8,128)(2,1)S(1)}, bf16[64,1024]{1,0:T(8,128)(2,1)S(1)}, u32[]{:S(2)}, u32[]{:S(2)}) collective-permute-start(bf16[64,1024]{1,0:T(8,128)(2,1)S(1)} %broadcast_select_fusion.2), channel_id=1, source_target_pairs={{0,2},{2,0},{1,3},{3,1},{4,6},{6,4},{5,7},{7,5},{8,10},{10,8},{9,1... | collective-permute-start | bytes 393224 | tf_op jit(solution)/shard_map/ppermute | solution.py:28
  256.7 15.4 %collective-permute-start.40 = (bf16[2,64,1024]{2,1,0:T(8,128)(2,1)S(1)}, bf16[2,64,1024]{2,1,0:T(8,128)(2,1)S(1)}, u32[]{:S(2)}, u32[]{:S(2)}) collective-permute-start(bf16[2,64,1024]{2,1,0:T(8,128)(2,1)S(1)} %get-tuple-element.142), channel_id=1, source_target_pairs={{0,4},{4,8},{8,12},{12,0},{1,5},{5,9},{9,13},{13,1},{2,6},{6,10},{... | collective-permute-start | bytes 786440 | tf_op jit(solution)/shard_map/ppermute | solution.py:33
  258.5 14.1 %collective-permute-start.42 = (bf16[2,64,1024]{2,1,0:T(8,128)(2,1)S(1)}, bf16[2,64,1024]{2,1,0:T(8,128)(2,1)S(1)}, u32[]{:S(2)}, u32[]{:S(2)}) collective-permute-start(bf16[2,64,1024]{2,1,0:T(8,128)(2,1)S(1)} %get-tuple-element.144), channel_id=1, source_target_pairs={{0,12},{4,0},{8,4},{12,8},{1,13},{5,1},{9,5},{13,9},{2,14},{6,2},{... | collective-permute-start | bytes 786440 | tf_op jit(solution)/shard_map/ppermute | solution.py:33
  261.4 16.4 %collective-permute-start.33 = (bf16[2,64,1152]{2,1,0:T(8,128)(2,1)S(1)}, bf16[2,64,1152]{2,1,0:T(8,128)(2,1)S(1)}, u32[]{:S(2)}, u32[]{:S(2)}) collective-permute-start(bf16[2,64,1152]{2,1,0:T(8,128)(2,1)S(1)} %get-tuple-element.136), channel_id=1, source_target_pairs={{0,16},{16,32},{32,48},{48,0},{1,17},{17,33},{33,49},{49,1},{2,18}... | collective-permute-start | bytes 884744 | tf_op jit(solution)/shard_map/ppermute | solution.py:33
  262.6 15.2 %collective-permute-start.35 = (bf16[2,64,1152]{2,1,0:T(8,128)(2,1)S(1)}, bf16[2,64,1152]{2,1,0:T(8,128)(2,1)S(1)}, u32[]{:S(2)}, u32[]{:S(2)}) collective-permute-start(bf16[2,64,1152]{2,1,0:T(8,128)(2,1)S(1)} %get-tuple-element.138), channel_id=1, source_target_pairs={{0,48},{16,0},{32,16},{48,32},{1,49},{17,1},{33,17},{49,33},{2,50}... | collective-permute-start | bytes 884744 | tf_op jit(solution)/shard_map/ppermute | solution.py:33
  272.9 25.4 %collective-permute-start.43 = (bf16[4,64,1024]{2,1,0:T(8,128)(2,1)S(1)}, bf16[4,64,1024]{2,1,0:T(8,128)(2,1)S(1)}, u32[]{:S(2)}, u32[]{:S(2)}) collective-permute-start(bf16[4,64,1024]{2,1,0:T(8,128)(2,1)S(1)} %pad_maximum_fusion.3), channel_id=1, source_target_pairs={{0,12},{4,0},{8,4},{12,8},{1,13},{5,1},{9,5},{13,9},{2,14},{6,2},{... | collective-permute-start | bytes 1572872 | tf_op jit(solution)/shard_map/ppermute | solution.py:33
  275.9 25.3 %collective-permute-start.41 = (bf16[4,64,1024]{2,1,0:T(8,128)(2,1)S(1)}, bf16[4,64,1024]{2,1,0:T(8,128)(2,1)S(1)}, u32[]{:S(2)}, u32[]{:S(2)}) collective-permute-start(bf16[4,64,1024]{2,1,0:T(8,128)(2,1)S(1)} %pad_maximum_fusion.2), channel_id=1, source_target_pairs={{0,4},{4,8},{8,12},{12,0},{1,5},{5,9},{9,13},{13,1},{2,6},{6,10},{... | collective-permute-start | bytes 1572872 | tf_op jit(solution)/shard_map/ppermute | solution.py:33
  278.1 26.7 %collective-permute-start.36 = (bf16[4,64,1152]{2,1,0:T(8,128)(2,1)S(1)}, bf16[4,64,1152]{2,1,0:T(8,128)(2,1)S(1)}, u32[]{:S(2)}, u32[]{:S(2)}) collective-permute-start(bf16[4,64,1152]{2,1,0:T(8,128)(2,1)S(1)} %pad_maximum_fusion.1), channel_id=1, source_target_pairs={{0,48},{16,0},{32,16},{48,32},{1,49},{17,1},{33,17},{49,33},{2,50}... | collective-permute-start | bytes 1769480 | tf_op jit(solution)/shard_map/ppermute | solution.py:33
  281.0 24.5 %collective-permute-start.34 = (bf16[4,64,1152]{2,1,0:T(8,128)(2,1)S(1)}, bf16[4,64,1152]{2,1,0:T(8,128)(2,1)S(1)}, u32[]{:S(2)}, u32[]{:S(2)}) collective-permute-start(bf16[4,64,1152]{2,1,0:T(8,128)(2,1)S(1)} %pad_maximum_fusion), channel_id=1, source_target_pairs={{0,16},{16,32},{32,48},{48,0},{1,17},{17,33},{33,49},{49,1},{2,18}... | collective-permute-start | bytes 1769480 | tf_op jit(solution)/shard_map/ppermute | solution.py:33
  281.9 38.1 %collective-permute-start.32 = (f32[64,1024]{1,0:T(8,128)S(1)}, f32[64,1024]{1,0:T(8,128)S(1)}, u32[]{:S(2)}, u32[]{:S(2)}) collective-permute-start(f32[64,1024]{1,0:T(8,128)S(1)} %dynamic-slice_select_fusion), channel_id=1, source_target_pairs={{0,2},{2,0},{1,3},{3,1},{4,6},{6,4},{5,7},{7,5},{8,10},{10,8},{9,1... | collective-permute-start | bytes 786440 | tf_op jit(solution)/shard_map/ppermute | solution.py:28
  301.5 6.7 %collective-permute-start.46 = (bf16[64,1024]{1,0:T(8,128)(2,1)S(1)}, bf16[64,1024]{1,0:T(8,128)(2,1)S(1)}, u32[]{:S(2)}, u32[]{:S(2)}) collective-permute-start(bf16[64,1024]{1,0:T(8,128)(2,1)S(1)} %get-tuple-element.152), channel_id=1, source_target_pairs={{0,48},{16,0},{32,16},{48,32},{1,49},{17,1},{33,17},{49,33},{2,50}... | collective-permute-start | bytes 393224 | tf_op jit(solution)/shard_map/ppermute | solution.py:33
  303.3 7.2 %collective-permute-start.45 = (bf16[64,1024]{1,0:T(8,128)(2,1)S(1)}, bf16[64,1024]{1,0:T(8,128)(2,1)S(1)}, u32[]{:S(2)}, u32[]{:S(2)}) collective-permute-start(bf16[64,1024]{1,0:T(8,128)(2,1)S(1)} %get-tuple-element.153), channel_id=1, source_target_pairs={{0,32},{16,48},{32,0},{48,16},{1,33},{17,49},{33,1},{49,17},{2,34}... | collective-permute-start | bytes 393224 | tf_op jit(solution)/shard_map/ppermute | solution.py:33
  304.8 7.0 %collective-permute-start.44 = (bf16[64,1024]{1,0:T(8,128)(2,1)S(1)}, bf16[64,1024]{1,0:T(8,128)(2,1)S(1)}, u32[]{:S(2)}, u32[]{:S(2)}) collective-permute-start(bf16[64,1024]{1,0:T(8,128)(2,1)S(1)} %get-tuple-element.151), channel_id=1, source_target_pairs={{0,16},{16,32},{32,48},{48,0},{1,17},{17,33},{33,49},{49,1},{2,18}... | collective-permute-start | bytes 393224 | tf_op jit(solution)/shard_map/ppermute | solution.py:33
  305.7 6.2 %collective-permute-start.39 = (bf16[64,1152]{1,0:T(8,128)(2,1)S(1)}, bf16[64,1152]{1,0:T(8,128)(2,1)S(1)}, u32[]{:S(2)}, u32[]{:S(2)}) collective-permute-start(bf16[64,1152]{1,0:T(8,128)(2,1)S(1)} %get-tuple-element.149), channel_id=1, source_target_pairs={{0,12},{4,0},{8,4},{12,8},{1,13},{5,1},{9,5},{13,9},{2,14},{6,2},{... | collective-permute-start | bytes 442376 | tf_op jit(solution)/shard_map/ppermute | solution.py:33
  308.2 6.6 %collective-permute-start.38 = (bf16[64,1152]{1,0:T(8,128)(2,1)S(1)}, bf16[64,1152]{1,0:T(8,128)(2,1)S(1)}, u32[]{:S(2)}, u32[]{:S(2)}) collective-permute-start(bf16[64,1152]{1,0:T(8,128)(2,1)S(1)} %get-tuple-element.150), channel_id=1, source_target_pairs={{0,8},{4,12},{8,0},{12,4},{1,9},{5,13},{9,1},{13,5},{2,10},{6,14},... | collective-permute-start | bytes 442376 | tf_op jit(solution)/shard_map/ppermute | solution.py:33
  310.5 7.8 %collective-permute-start.37 = (bf16[64,1152]{1,0:T(8,128)(2,1)S(1)}, bf16[64,1152]{1,0:T(8,128)(2,1)S(1)}, u32[]{:S(2)}, u32[]{:S(2)}) collective-permute-start(bf16[64,1152]{1,0:T(8,128)(2,1)S(1)} %get-tuple-element.148), channel_id=1, source_target_pairs={{0,4},{4,8},{8,12},{12,0},{1,5},{5,9},{9,13},{13,1},{2,6},{6,10},{... | collective-permute-start | bytes 442376 | tf_op jit(solution)/shard_map/ppermute | solution.py:33
  318.4 6.7 %collective-permute-start.47 = (bf16[64,1152]{1,0:T(8,128)(2,1)S(1)}, bf16[64,1152]{1,0:T(8,128)(2,1)S(1)}, u32[]{:S(2)}, u32[]{:S(2)}) collective-permute-start(bf16[64,1152]{1,0:T(8,128)(2,1)S(1)} %pad_maximum_fusion.8), channel_id=1, source_target_pairs={{0,2},{2,0},{1,3},{3,1},{4,6},{6,4},{5,7},{7,5},{8,10},{10,8},{9,1... | collective-permute-start | bytes 442376 | tf_op jit(solution)/shard_map/ppermute | solution.py:28
  332.4 5.8 %collective-permute-start.49 = (bf16[64,512]{1,0:T(8,128)(2,1)S(1)}, bf16[64,512]{1,0:T(8,128)(2,1)S(1)}, u32[]{:S(2)}, u32[]{:S(2)}) collective-permute-start(bf16[64,512]{1,0:T(8,128)(2,1)S(1)} %slice_select_fusion), channel_id=1, source_target_pairs={{0,2},{2,0},{1,3},{3,1},{4,6},{6,4},{5,7},{7,5},{8,10},{10,8},{9,1... | collective-permute-start | bytes 196616 | tf_op jit(solution)/shard_map/ppermute | solution.py:28
  339.1 4.3 %collective-permute-start.50 = (bf16[32,512]{1,0:T(8,128)(2,1)S(1)}, bf16[32,512]{1,0:T(8,128)(2,1)S(1)}, u32[]{:S(2)}, u32[]{:S(2)}) collective-permute-start(bf16[32,512]{1,0:T(8,128)(2,1)S(1)} %select_convert_fusion), channel_id=1, source_target_pairs={{0,64},{64,0},{1,65},{65,1},{2,66},{66,2},{3,67},{67,3},{4,68},{68... | collective-permute-start | bytes 98312 | tf_op jit(solution)/shard_map/ppermute | solution.py:28
  341.0 8.0 %collective-permute-start.48 = (bf16[64,2048]{1,0:T(8,128)(2,1)S(1)}, bf16[64,2048]{1,0:T(8,128)(2,1)S(1)}, u32[]{:S(2)}, u32[]{:S(2)}) collective-permute-start(bf16[64,2048]{1,0:T(8,128)(2,1)S(1)} %pad_maximum_fusion.7), channel_id=1, source_target_pairs={{0,2},{2,0},{1,3},{3,1},{4,6},{6,4},{5,7},{7,5},{8,10},{10,8},{9,1... | collective-permute-start | bytes 786440 | tf_op jit(solution)/shard_map/ppermute | solution.py:28
  (45 other events, 402.2 us)
Sparse Core Ops, SparseCore 0:
  27.8 97.0 all-gather.1
  228.8 101.9 reduce-scatter.1
